TPU v7x, 32 devices: a whole 2x2x4 slice. The times are simulated.
32 devices in a mesh: gx: 4 (over y, x), gy: 2 (over core), gz: 4 (over z).
Axes of the slice: x: 2, y: 2, z: 4, core: 2. Of those that a mesh axis runs over, the one named last changes fastest.
Arguments:
- field: float32 [4, 2048, 512], P(None, ('gx', 'gy', 'gz')), may hold values from -6 to 6
- neighbours: int32 [2048, 6], P(('gx', 'gy', 'gz')), may hold values from -1 to 2047, as said below
- cell_one: int32 [65536], P(('gx', 'gy', 'gz')), may hold values from 0 to 2047, as said below
- ref_one: float32 [3, 65536], P(None, ('gx', 'gy', 'gz')), may hold values from -1 to 1
- cell_two: int32 [65536], P(('gx', 'gy', 'gz')), may hold values from 0 to 2047, as said below
- ref_two: float32 [3, 65536], P(None, ('gx', 'gy', 'gz')), may hold values from -1 to 1
- velocity: float32 [3, 65536], P(None, ('gx', 'gy', 'gz')), may hold values from -6 to 6
- rate: float32 [65536], P(('gx', 'gy', 'gz')), may hold values from 0.5 to 8
- cut: int32 [1], replicated, may hold values from 1 to 2047
Outputs:
- field_out: float32 [4, 2048, 512], P(None, ('gx', 'gy', 'gz'))
- velocity_out: float32 [3, 65536], P(None, ('gx', 'gy', 'gz'))
Inputs may be any that keep to these rules, and one draw needn't show every extreme that they name: `neighbours`: across face f of an element lies an element of the same device or of the adjacent device along that face's axis (cyclic along gz), with the same face node order; -1 marks walls at the ends along gx and gy. The order of elements within a device is arbitrary. `cell_one`: A particle's element is owned by a device with the same gx index as its bin. From one bin at most 512 particles lie in the elements of one device, and in each slab one device receives exactly 512 from every bin of the slab. `cell_two`: as for cell_one, for the second step's bins.
All inputs are finite; a program needn't handle non-finite values.
Results may differ from a plain program's by a relative error of at most 0.0003.
Values sent between devices are 32-bit elements; how exact they have to be, the bound alone decides.
A program may use at most 128 MiB of HBM per device.

v0:
```python
import jax
import jax.numpy as jnp
import numpy as np
from jax import lax
from jax.sharding import PartitionSpec as P

EDGE = 4


node_points = -np.cos(np.pi * np.arange(8) / 7.0)
step_time = 0.1
viscosity = 0.002
penalty = 0.25
loading = 0.5
heating = 0.5
highest = lax.Precision.HIGHEST


def from_behind(block, axis, distance):
    devices = range(lax.axis_size(axis))
    route = [(i - distance, i) for i in devices if i - distance in devices]
    return lax.ppermute(block, axis, route)


def shifted(block, axis, distance):
    devices = range(lax.axis_size(axis))
    route = [((i - distance) % len(devices), i) for i in devices]
    return lax.ppermute(block, axis, route)


def gap_table():
    differences = node_points[:, None] - node_points[None, :] + np.eye(8)
    inverse = 1.0 / differences
    return inverse * (1.0 - np.eye(8))


def laplace_table():
    differences = node_points[:, None] - node_points[None, :] + np.eye(8)
    weights = 1.0 / np.prod(differences, axis=1)
    derivative = weights[None, :] / weights[:, None] / differences
    derivative = derivative * (1.0 - np.eye(8))
    derivative = derivative - np.eye(8) * derivative.sum(axis=1)[:, None]
    second = derivative @ derivative
    identity = np.eye(8)
    operator = np.kron(np.kron(second, identity), identity)
    operator = operator + np.kron(np.kron(identity, second), identity)
    operator = operator + np.kron(np.kron(identity, identity), second)
    return operator.T


def face_table():
    selection = np.zeros((512, 384))
    for face_side in range(6):
        edge_value = 0 if face_side % 2 == 0 else 7
        for row_node in range(8):
            for col_node in range(8):
                if face_side < 2:
                    node_index = (edge_value * 8 + row_node) * 8 + col_node
                elif face_side < 4:
                    node_index = (row_node * 8 + edge_value) * 8 + col_node
                else:
                    node_index = (row_node * 8 + col_node) * 8 + edge_value
                selection[node_index, face_side * 64 + row_node * 8 + col_node] = 1.0
    return selection


def transfer_table(face_side):
    selection = face_table()
    partner_cols = selection[:, (face_side ^ 1) * 64 : ((face_side ^ 1) + 1) * 64]
    own_cols = selection[:, face_side * 64 : (face_side + 1) * 64]
    return partner_cols @ own_cols.T


def expand_table(direction):
    positions = np.arange(512)
    digits = positions // 8 ** (2 - direction) % 8
    return np.where(digits[None, :] == np.arange(8)[:, None], 1.0, 0.0)


def lagrange(coordinate):
    points = jnp.asarray(node_points, jnp.float32)
    inverse = jnp.asarray(gap_table(), jnp.float32)
    identity = jnp.eye(8, dtype=jnp.float32)
    offsets = coordinate[:, None] - points[None, :]
    factors = offsets[:, None, :] * inverse[None, :, :] + identity[None, :, :]
    return jnp.prod(factors, axis=2)


def basis(coords):
    result = None
    for direction in range(3):
        spread = jnp.dot(
            lagrange(coords[direction]),
            jnp.asarray(expand_table(direction), jnp.float32),
            precision=highest,
        )
        result = spread if result is None else result * spread
    return result


def local(field, neighbours, cell_one, ref_one, cell_two, ref_two, velocity, rate, cut):
    count_y = lax.axis_size("gy")
    count_z = lax.axis_size("gz")
    owners = count_y * count_z
    elements = field.shape[1]
    particles = cell_one.shape[0]
    capacity = 2 * particles // owners
    slots = owners * capacity
    edge_cells = EDGE * EDGE
    device_here = lax.axis_index(("gx", "gy", "gz"))
    selection = jnp.asarray(face_table(), jnp.float32)
    laplace_matrix = jnp.asarray(laplace_table(), jnp.float32)
    transfers = [jnp.asarray(transfer_table(side), jnp.float32) for side in range(6)]
    multiplicity = jnp.asarray(face_table().sum(axis=1), jnp.float32)
    coupling = jnp.asarray([-loading, -loading, -loading, heating], jnp.float32)
    positions = jnp.arange(elements, dtype=jnp.int32)
    outer_order = []
    far_rank = []
    for side in range(6):
        target = neighbours[:, side]
        outside = (target < 0) | (target // elements != device_here)
        keyed = jnp.where(outside, positions, elements + positions)
        outer_order.append(jnp.argsort(keyed)[:edge_cells])
        remote = (target >= 0) & (target // elements != device_here)
        slot_key = jnp.where(remote, jnp.maximum(target, 0) % elements, elements)
        ranked = jnp.sum((slot_key[None, :] < slot_key[:, None]).astype(jnp.int32), axis=1)
        far_rank.append(jnp.minimum(ranked, edge_cells - 1))

    def surface_jump(state):
        compact = []
        for side in range(6):
            rows = state[:, outer_order[side], :].reshape(-1, 512)
            picked = jnp.dot(rows, selection[:, side * 64 : (side + 1) * 64], precision=highest)
            compact.append(picked.reshape(4, edge_cells * 64))
        arrived = [
            from_behind(compact[1], "gx", 1),
            from_behind(compact[0], "gx", -1),
            from_behind(compact[3], "gy", 1),
            from_behind(compact[2], "gy", -1),
            shifted(compact[5], "gz", 1),
            shifted(compact[4], "gz", -1),
        ]
        total = -state * multiplicity[None, None, :]
        for side in range(6):
            target = neighbours[:, side]
            local_slot = jnp.maximum(target, 0) % elements
            on_device = target // elements == device_here
            present = target >= 0
            own_rows = state[:, local_slot, :].reshape(-1, 512)
            own_side = jnp.dot(own_rows, transfers[side], precision=highest).reshape(
                4, elements, 512
            )
            widened = jnp.dot(
                arrived[side].reshape(4 * edge_cells, 64),
                selection[:, side * 64 : (side + 1) * 64].T,
                precision=highest,
            ).reshape(4, edge_cells, 512)
            far_side = widened[:, far_rank[side], :]
            partner = jnp.where(on_device[None, :, None], own_side, far_side)
            partner = jnp.where(present[None, :, None], partner, jnp.zeros_like(partner))
            total = total + partner
        return total

    def send_out(outgoing):
        shaped = outgoing.reshape(8, owners, capacity)
        moved = lax.all_to_all(shaped, ("gy", "gz"), split_axis=1, concat_axis=1, tiled=True)
        return moved.reshape(8, slots)

    def send_back(values):
        shaped = values.reshape(3, owners, capacity)
        moved = lax.all_to_all(shaped, ("gy", "gz"), split_axis=1, concat_axis=1, tiled=True)
        return moved.reshape(3, slots)

    def coupled_step(state, cells, coords, speeds, rates):
        owner = cells // elements % owners
        element = cells % elements
        marks = (owner[:, None] == jnp.arange(owners, dtype=jnp.int32)[None, :]).astype(jnp.int32)
        rank = jnp.sum(marks * (jnp.cumsum(marks, axis=0) - 1), axis=1)
        slot = owner * capacity + rank
        payload = jnp.concatenate(
            [element.astype(jnp.float32)[None], coords, speeds, rates[None]], axis=0
        )
        outgoing = jnp.zeros((8, slots), jnp.float32).at[0].set(-1.0).at[:, slot].set(payload)
        incoming = send_out(outgoing)
        jump = surface_jump(state)
        laplace = jnp.dot(state.reshape(-1, 512), laplace_matrix, precision=highest).reshape(
            state.shape
        )
        blocks = slots // 512

        def visit(block_index, carry):
            force, fresh_all = carry
            start = block_index * 512
            piece = lax.dynamic_slice_in_dim(incoming, start, 512, 1)
            index = jnp.maximum(piece[0], 0.0).astype(jnp.int32)
            weights = basis(piece[1:4])
            speed_block = piece[4:7]
            rate_block = piece[7]
            pick = (index[:, None] == jnp.arange(elements, dtype=jnp.int32)[None, :]).astype(
                jnp.float32
            )
            fluid = jnp.stack(
                [
                    jnp.sum(jnp.dot(pick, state[component], precision=highest) * weights, axis=1)
                    for component in range(3)
                ]
            )
            offset_block = fluid - speed_block
            accel = rate_block[None] * offset_block
            heat = rate_block * jnp.sum(offset_block * offset_block, axis=0)
            fresh = speed_block + step_time * accel
            sources = [accel[0], accel[1], accel[2], heat]
            added = jnp.stack(
                [
                    jnp.einsum(
                        "pe,pn->en", pick, sources[component][:, None] * weights, precision=highest
                    )
                    for component in range(4)
                ]
            )
            fresh_all = lax.dynamic_update_slice_in_dim(fresh_all, fresh, start, 1)
            return (force + added, fresh_all)

        force, fresh_all = lax.fori_loop(
            0,
            blocks,
            visit,
            (jnp.zeros(state.shape, jnp.float32), jnp.zeros((3, slots), jnp.float32)),
        )
        returned = send_back(fresh_all)
        new_speeds = returned[:, slot]
        new_state = state + viscosity * laplace + penalty * jump + coupling[:, None, None] * force
        return (new_state, new_speeds)

    first_state, first_speeds = coupled_step(field, cell_one, ref_one, velocity, rate)
    carried = jnp.concatenate([first_speeds, rate[None]], axis=0)
    following = shifted(carried, ("gy", "gz"), -1)
    doubled = jnp.concatenate([carried, following], axis=1)
    moved = lax.dynamic_slice_in_dim(doubled, cut[0], particles, 1)
    final_state, final_speeds = coupled_step(first_state, cell_two, ref_two, moved[:3], moved[3])
    return (final_state, final_speeds)


def solution(mesh):
    in_specs = (
        P(None, ("gx", "gy", "gz"), None),
        P(("gx", "gy", "gz"), None),
        P(("gx", "gy", "gz")),
        P(None, ("gx", "gy", "gz")),
        P(("gx", "gy", "gz")),
        P(None, ("gx", "gy", "gz")),
        P(None, ("gx", "gy", "gz")),
        P(("gx", "gy", "gz")),
        P(),
    )
    out_specs = (P(None, ("gx", "gy", "gz"), None), P(None, ("gx", "gy", "gz")))
    return jax.shard_map(local, mesh=mesh, in_specs=in_specs, out_specs=out_specs, check_vma=False)
```

profile of v0, /device:TPU:5, one launch (start us, length us, event | category | flops | bytes accessed | tf_op | source)
XLA Modules:
  0.0 396.5 jit_solution(11949526430307295608)
XLA Ops:
  1.5 1.5 bitcast_compare_fusion
  4.0 2.0 sort.87
  6.0 1.6 gather_fusion.1
  8.9 3.1 collective-permute-start
  12.0 2.0 sort.88
  15.2 3.1 collective-permute-start.1
  18.3 2.0 sort.89
  22.8 2.0 sort.90
  24.8 2.0 sort.92
  28.0 3.1 collective-permute-start.3
  31.1 2.0 sort.91
  35.7 2.3 reduce-window.14
  40.5 1.6 copy.319
  43.5 6.7 %scatter_fusion = f32[8,4096]{0,1:T(8,128)S(1)} fusion(f32[8,4096]{0,1:T(8,128)S(1)} %copy.319, s32[2048]{0:T(1024)S(1)} %get-tuple-element.695, f32[2048,8]{1,0:T(8,128)} %copy.223), kind=kCustom, calls=%fused_computation.38 | custom fusion | bytes 204800 | tf_op jit(solution)/shard_map/scatter | solution.py:183
  51.5 4.2 %all-to-all-start = ((f32[8,8,512]{2,0,1:T(8,128)}), f32[8,8,512]{2,0,1:T(8,128)}, u32[]{:S(2)}, u32[]{:S(2)}) async-start(f32[8,8,512]{2,0,1:T(8,128)} %copy.224), calls=%async_computation | async-start | bytes 262144 | tf_op jit(solution)/shard_map/all_to_all | solution.py:166
  60.8 2.3 reduce-window.16
  64.6 2.1 gather_fusion
  66.7 2.1 gather_fusion.3
  68.8 2.1 gather_fusion.6
  70.9 2.1 gather_fusion.9
  73.0 2.1 gather_fusion.12
  75.3 2.1 gather_fusion.15
  78.1 3.4 collective-permute-start.5
  84.4 1.6 gather_fusion.2
  86.0 1.6 gather_fusion.5
  87.6 1.9 gather_fusion.8
  89.5 1.8 gather_fusion.11
  91.3 1.9 gather_fusion.14
  93.2 1.6 gather_fusion.17
  94.8 2.4 fusion.92
  102.8 1.9 fusion.82
  104.8 86.3 %while.38 = (s32[]{:T(128)}, f32[4,64,512]{2,1,0:T(8,128)S(1)}, f32[3,4096]{1,0:T(4,128)S(1)}, f32[8,4096]{1,0:T(8,128)}, f32[4,64,512]{2,1,0:T(8,128)S(1)}, /*i...) while((s32[]{:T(128)}, f32[4,64,512]{2,1,0:T(8,128)S(1)}, ...), condition=%wide.region_24.25_spmd.clone.clone.clone, body=%wide.region_16.24_spmd.sunk.clone.clone.clone.sunk | while | flops 1489251968 | bytes 15426653 | solution.py:224
  191.1 2.5 fusion.94
  197.8 1.7 gather_fusion.21
  201.0 1.7 gather_fusion.24
  203.5 1.9 gather_fusion.27
  206.2 1.9 gather_fusion.30
  209.0 1.9 gather_fusion.33
  210.9 5.2 %all-to-all-start.1 = ((f32[3,8,512]{2,0,1:T(4,128)}), f32[3,8,512]{2,0,1:T(4,128)S(1)}, u32[]{:S(2)}, u32[]{:S(2)}) async-start(f32[3,8,512]{2,0,1:T(4,128)} %bitcast.585), calls=%async_computation.1 | async-start | bytes 131072 | tf_op jit(solution)/shard_map/all_to_all | solution.py:171
  218.0 1.5 reshape.1114
  219.5 2.2 collective-permute-start.6
  224.4 3.9 collective-permute-start.7
  229.7 1.5 collective-permute-start.8
  231.5 3.0 collective-permute-start.9
  238.0 1.9 collective-permute-start.11
  244.6 1.7 gather_fusion.23
  247.4 1.8 gather_fusion.26
  250.1 1.8 gather_fusion.29
  254.0 1.8 gather_fusion.32
  261.4 2.0 fusion.71
  264.3 2.0 copy.261
  266.2 7.1 %gather_fusion.36 = f32[2048,3]{1,0:T(8,128)S(1)} fusion(f32[3,4096]{0,1:T(8,128)} %bitcast.552, s32[2048]{0:T(1024)S(1)} %copy-done.65), kind=kCustom, calls=%fused_computation.36 | custom fusion | bytes 57344 | tf_op jit(solution)/shard_map/gather | solution.py:231
  273.7 1.5 collective-permute-start.12
  275.5 1.7 gather_fusion.35
  278.8 8.8 %scatter_fusion.1 = f32[8,4096]{0,1:T(8,128)} fusion(f32[8,4096]{0,1:T(8,128)} %copy.307, s32[2048]{0:T(1024)S(1)} %copy-done.61, f32[2048,8]{1,0:T(8,128)} %copy.263), kind=kCustom, calls=%fused_computation.39 | custom fusion | bytes 204800 | tf_op jit(solution)/shard_map/scatter | solution.py:183
  287.6 2.8 copy.264
  290.5 4.9 %all-to-all-start.2 = ((f32[8,8,512]{2,0,1:T(8,128)}), f32[8,8,512]{2,0,1:T(8,128)S(1)}, u32[]{:S(2)}, u32[]{:S(2)}) async-start(f32[8,8,512]{2,0,1:T(8,128)} %copy.264), calls=%async_computation.2 | async-start | bytes 262144 | tf_op jit(solution)/shard_map/all_to_all | solution.py:166
  295.4 2.5 fusion.69
  297.9 4.1 %all-to-all-done.2 = f32[8,8,512]{2,0,1:T(8,128)S(1)} async-done(((f32[8,8,512]{2,0,1:T(8,128)}), f32[8,8,512]{2,0,1:T(8,128)S(1)}, u32[]{:S(2)}, u32[]{:S(2)}) %all-to-all-start.2) | async-done | bytes 131104 | tf_op jit(solution)/shard_map/all_to_all | solution.py:166
  302.6 77.4 %while.39 = (s32[]{:T(128)}, f32[4,64,512]{2,1,0:T(8,128)S(1)}, f32[3,4096]{1,0:T(4,128)}, f32[8,4096]{1,0:T(8,128)S(1)}, f32[4,64,512]{2,1,0:T(8,128)S(1)}, /*i...) while((s32[]{:T(128)}, f32[4,64,512]{2,1,0:T(8,128)S(1)}, ...), condition=%wide.region_37.38_spmd.clone.clone.clone, body=%wide.region_29.37_spmd.sunk.clone.clone.clone.sunk | while | flops 1489251968 | bytes 15424605 | solution.py:224
  380.0 3.7 all-to-all-start.3
  383.6 3.1 fusion.93
  386.8 2.5 all-to-all-done.3
  389.9 5.5 %gather_fusion.37 = f32[2048,3]{1,0:T(8,128)S(1)} fusion(f32[3,4096]{0,1:T(8,128)S(1)} %bitcast.553, s32[2048]{0:T(1024)S(1)} %copy-done.64), kind=kCustom, calls=%fused_computation.37 | custom fusion | bytes 57344 | tf_op jit(solution)/shard_map/gather | solution.py:231
  (690 shorter events, 228.6 us)
Async XLA Ops:
  0.6 14.2 %copy-start.54 = (f32[512,64]{0,1:T(8,128)S(1)}, f32[512,64]{0,1:T(8,128)}, u32[]{:S(2)}) copy-start(f32[512,64]{0,1:T(8,128)} %constant.458) | copy-start | bytes 393220
  0.6 13.4 %copy-start = (f32[4,64,512]{2,1,0:T(8,128)S(1)}, f32[4,64,512]{2,1,0:T(8,128)}, u32[]{:S(2)}) copy-start(f32[4,64,512]{2,1,0:T(8,128)} %param.45) | copy-start | bytes 1572868
  6.0 15.1 %copy-start.52 = (f32[512,64]{0,1:T(8,128)S(1)}, f32[512,64]{0,1:T(8,128)}, u32[]{:S(2)}) copy-start(f32[512,64]{0,1:T(8,128)} %constant.459) | copy-start | bytes 393220
  8.9 69.2 %collective-permute-start = (f32[4,1024]{1,0:T(4,128)S(1)}, f32[4,1024]{1,0:T(4,128)S(1)}, u32[]{:S(2)}, u32[]{:S(2)}) collective-permute-start(f32[4,1024]{1,0:T(4,128)S(1)} %reshape.1099), channel_id=1, source_target_pairs={{0,8},{8,16},{16,24},{1,9},{9,17},{17,25},{2,10},{10,18},{18,26},{... | collective-permute-start | bytes 49160 | tf_op jit(solution)/shard_map/ppermute | solution.py:22
  14.1 13.6 %copy-start.50 = (f32[512,64]{0,1:T(8,128)S(1)}, f32[512,64]{0,1:T(8,128)}, u32[]{:S(2)}) copy-start(f32[512,64]{0,1:T(8,128)} %constant.460) | copy-start | bytes 393220
  15.2 66.7 %collective-permute-start.1 = (f32[4,1024]{1,0:T(4,128)S(1)}, f32[4,1024]{1,0:T(4,128)S(1)}, u32[]{:S(2)}, u32[]{:S(2)}) collective-permute-start(f32[4,1024]{1,0:T(4,128)S(1)} %reshape.1101), channel_id=1, source_target_pairs={{8,0},{16,8},{24,16},{9,1},{17,9},{25,17},{10,2},{18,10},{26,18},{... | collective-permute-start | bytes 49160 | tf_op jit(solution)/shard_map/ppermute | solution.py:22
  20.3 13.6 %copy-start.48 = (f32[512,64]{0,1:T(8,128)S(1)}, f32[512,64]{0,1:T(8,128)}, u32[]{:S(2)}) copy-start(f32[512,64]{0,1:T(8,128)} %constant.461) | copy-start | bytes 393220
  20.3 15.3 %copy-start.70 = (s32[2048]{0:T(1024)S(1)}, s32[2048]{0:T(1024)}, u32[]{:S(2)}) copy-start(s32[2048]{0:T(1024)} %param.47) | copy-start | bytes 24580
  21.1 18.1 %copy-start.59 = (f32[2048]{0:T(1024)S(1)}, f32[2048]{0:T(1024)}, u32[]{:S(2)}) copy-start(f32[2048]{0:T(1024)} %param.52) | copy-start | bytes 24580
  21.1 18.1 %copy-start.66 = (f32[3,2048]{1,0:T(4,128)S(1)}, f32[3,2048]{1,0:T(4,128)}, u32[]{:S(2)}) copy-start(f32[3,2048]{1,0:T(4,128)} %param.51) | copy-start | bytes 73732
  21.1 18.1 %copy-start.67 = (f32[3,2048]{1,0:T(4,128)S(1)}, f32[3,2048]{1,0:T(4,128)}, u32[]{:S(2)}) copy-start(f32[3,2048]{1,0:T(4,128)} %param.48) | copy-start | bytes 73732
  21.5 60.8 %collective-permute-start.2 = (f32[4,1024]{1,0:T(4,128)S(1)}, f32[4,1024]{1,0:T(4,128)S(1)}, u32[]{:S(2)}, u32[]{:S(2)}) collective-permute-start(f32[4,1024]{1,0:T(4,128)S(1)} %reshape.1103), channel_id=1, source_target_pairs={{0,4},{1,5},{2,6},{3,7},{8,12},{9,13},{10,14},{11,15},{16,20},{17,... | collective-permute-start | bytes 49160 | tf_op jit(solution)/shard_map/ppermute | solution.py:22
  26.9 11.1 %copy-start.78 = (s32[1024]{0:T(1024)}, s32[1024]{0:T(1024)S(1)}, u32[]{:S(2)}) copy-start(s32[1024]{0:T(1024)S(1)} %pad_clamp_fusion.7) | copy-start | bytes 12292
  28.0 54.7 %collective-permute-start.3 = (f32[4,1024]{1,0:T(4,128)S(1)}, f32[4,1024]{1,0:T(4,128)S(1)}, u32[]{:S(2)}, u32[]{:S(2)}) collective-permute-start(f32[4,1024]{1,0:T(4,128)S(1)} %reshape.1105), channel_id=1, source_target_pairs={{4,0},{5,1},{6,2},{7,3},{12,8},{13,9},{14,10},{15,11},{20,16},{21,... | collective-permute-start | bytes 49160 | tf_op jit(solution)/shard_map/ppermute | solution.py:22
  34.3 48.7 %collective-permute-start.4 = (f32[4,1024]{1,0:T(4,128)S(1)}, f32[4,1024]{1,0:T(4,128)S(1)}, u32[]{:S(2)}, u32[]{:S(2)}) collective-permute-start(f32[4,1024]{1,0:T(4,128)S(1)} %reshape.1107), channel_id=1, source_target_pairs={{3,0},{0,1},{1,2},{2,3},{7,4},{4,5},{5,6},{6,7},{11,8},{8,9},{9,10... | collective-permute-start | bytes 49160 | tf_op jit(solution)/shard_map/ppermute | solution.py:28
  43.5 12.2 %copy-start.68 = (s32[64,6]{0,1:T(8,128)S(1)}, s32[64,6]{0,1:T(8,128)}, u32[]{:S(2)}) copy-start(s32[64,6]{0,1:T(8,128)} %param.46) | copy-start | bytes 4612
  50.2 9.9 %copy-start.71 = (s32[2048]{0:T(1024)S(1)}, s32[2048]{0:T(1024)}, u32[]{:S(2)}) copy-start(s32[2048]{0:T(1024)} %param.49) | copy-start | bytes 24580
  50.2 14.1 %copy-start.46 = (f32[512,64]{0,1:T(8,128)S(1)}, f32[512,64]{0,1:T(8,128)}, u32[]{:S(2)}) copy-start(f32[512,64]{0,1:T(8,128)} %constant.462) | copy-start | bytes 393220
  51.5 53.2 %all-to-all-start = ((f32[8,8,512]{2,0,1:T(8,128)}), f32[8,8,512]{2,0,1:T(8,128)}, u32[]{:S(2)}, u32[]{:S(2)}) async-start(f32[8,8,512]{2,0,1:T(8,128)} %copy.224), calls=%async_computation | async-start | bytes 262144 | tf_op jit(solution)/shard_map/all_to_all | solution.py:166
  56.5 27.9 %copy-start.76 = (s32[1024]{0:T(1024)}, s32[1024]{0:T(1024)S(1)}, u32[]{:S(2)}) copy-start(s32[1024]{0:T(1024)S(1)} %pad_clamp_fusion.15) | copy-start | bytes 12292
  56.5 10.2 %copy-start.80 = (s32[1024]{0:T(1024)}, s32[1024]{0:T(1024)S(1)}, u32[]{:S(2)}) copy-start(s32[1024]{0:T(1024)S(1)} %pad_clamp_fusion.17) | copy-start | bytes 12292
  56.7 29.3 %copy-start.77 = (s32[1024]{0:T(1024)}, s32[1024]{0:T(1024)S(1)}, u32[]{:S(2)}) copy-start(s32[1024]{0:T(1024)S(1)} %pad_clamp_fusion.12) | copy-start | bytes 12292
  56.7 10.0 %copy-start.81 = (s32[1024]{0:T(1024)}, s32[1024]{0:T(1024)S(1)}, u32[]{:S(2)}) copy-start(s32[1024]{0:T(1024)S(1)} %pad_clamp_fusion.14) | copy-start | bytes 12292
  57.5 11.3 %copy-start.82 = (s32[1024]{0:T(1024)}, s32[1024]{0:T(1024)S(1)}, u32[]{:S(2)}) copy-start(s32[1024]{0:T(1024)S(1)} %pad_clamp_fusion.11) | copy-start | bytes 12292
  58.3 12.6 %copy-start.83 = (s32[1024]{0:T(1024)}, s32[1024]{0:T(1024)S(1)}, u32[]{:S(2)}) copy-start(s32[1024]{0:T(1024)S(1)} %pad_clamp_fusion.8) | copy-start | bytes 12292
  59.2 13.9 %copy-start.84 = (s32[1024]{0:T(1024)}, s32[1024]{0:T(1024)S(1)}, u32[]{:S(2)}) copy-start(s32[1024]{0:T(1024)S(1)} %pad_clamp_fusion.5) | copy-start | bytes 12292
  59.4 33.8 %copy-start.73 = (s32[1024]{0:T(1024)}, s32[1024]{0:T(1024)S(1)}, u32[]{:S(2)}) copy-start(s32[1024]{0:T(1024)S(1)} %pad_clamp_fusion) | copy-start | bytes 12292
  64.5 10.7 %copy-start.86 = (s32[1024]{0:T(1024)}, s32[1024]{0:T(1024)S(1)}, u32[]{:S(2)}) copy-start(s32[1024]{0:T(1024)S(1)} %pad_clamp_fusion.2) | copy-start | bytes 12292
  75.3 7.1 %copy-start.40 = (f32[512,64,1]{0,1,2:T(8,128)S(1)}, f32[512,64,1]{0,1,2:T(8,128)}, u32[]{:S(2)}) copy-start(f32[512,64,1]{0,1,2:T(8,128)} %constant.483) | copy-start | bytes 393220
  75.3 7.5 %copy-start.38 = (f32[512,64,1]{0,1,2:T(8,128)S(1)}, f32[512,64,1]{0,1,2:T(8,128)}, u32[]{:S(2)}) copy-start(f32[512,64,1]{0,1,2:T(8,128)} %constant.485) | copy-start | bytes 393220
  75.3 7.8 %copy-start.37 = (f32[512,64,1]{0,1,2:T(8,128)S(1)}, f32[512,64,1]{0,1,2:T(8,128)}, u32[]{:S(2)}) copy-start(f32[512,64,1]{0,1,2:T(8,128)} %constant.487) | copy-start | bytes 393220
  78.1 5.8 %collective-permute-start.5 = (f32[4,1024]{1,0:T(4,128)S(1)}, f32[4,1024]{1,0:T(4,128)S(1)}, u32[]{:S(2)}, u32[]{:S(2)}) collective-permute-start(f32[4,1024]{1,0:T(4,128)S(1)} %reshape.1109), channel_id=1, source_target_pairs={{1,0},{2,1},{3,2},{0,3},{5,4},{6,5},{7,6},{4,7},{9,8},{10,9},{11,1... | collective-permute-start | bytes 49160 | tf_op jit(solution)/shard_map/ppermute | solution.py:28
  87.6 7.2 %copy-start.1 = (f32[512,512,1]{1,0,2:T(8,128)S(1)}, f32[512,512,1]{1,0,2:T(8,128)}, u32[]{:S(2)}) copy-start(f32[512,512,1]{1,0,2:T(8,128)} %constant.478) | copy-start | bytes 3145732
  87.6 7.2 %copy-start.69 = (f32[512]{0:T(512)S(1)}, f32[512]{0:T(512)}, u32[]{:S(2)}) copy-start(f32[512]{0:T(512)} %constant.450.clone) | copy-start | bytes 6148
  203.4 13.7 %copy-start.56 = (f32[512,64]{0,1:T(8,128)S(1)}, f32[512,64]{0,1:T(8,128)}, u32[]{:S(2)}) copy-start(f32[512,64]{0,1:T(8,128)} %constant.457) | copy-start | bytes 393220
  203.5 19.2 %copy-start.55 = (f32[512,64]{0,1:T(8,128)S(1)}, f32[512,64]{0,1:T(8,128)}, u32[]{:S(2)}) copy-start(f32[512,64]{0,1:T(8,128)} %constant.458) | copy-start | bytes 393220
  205.3 24.0 %copy-start.53 = (f32[512,64]{0,1:T(8,128)S(1)}, f32[512,64]{0,1:T(8,128)}, u32[]{:S(2)}) copy-start(f32[512,64]{0,1:T(8,128)} %constant.459) | copy-start | bytes 393220
  206.2 24.9 %copy-start.51 = (f32[512,64]{0,1:T(8,128)S(1)}, f32[512,64]{0,1:T(8,128)}, u32[]{:S(2)}) copy-start(f32[512,64]{0,1:T(8,128)} %constant.460) | copy-start | bytes 393220
  208.1 26.5 %copy-start.49 = (f32[512,64]{0,1:T(8,128)S(1)}, f32[512,64]{0,1:T(8,128)}, u32[]{:S(2)}) copy-start(f32[512,64]{0,1:T(8,128)} %constant.461) | copy-start | bytes 393220
  209.0 28.0 %copy-start.47 = (f32[512,64]{0,1:T(8,128)S(1)}, f32[512,64]{0,1:T(8,128)}, u32[]{:S(2)}) copy-start(f32[512,64]{0,1:T(8,128)} %constant.462) | copy-start | bytes 393220
  210.9 29.8 %copy-start.45 = (f32[512,64,1]{0,1,2:T(8,128)S(1)}, f32[512,64,1]{0,1,2:T(8,128)}, u32[]{:S(2)}) copy-start(f32[512,64,1]{0,1,2:T(8,128)} %constant.479) | copy-start | bytes 393220
  210.9 30.1 %copy-start.43 = (f32[512,64,1]{0,1,2:T(8,128)S(1)}, f32[512,64,1]{0,1,2:T(8,128)}, u32[]{:S(2)}) copy-start(f32[512,64,1]{0,1,2:T(8,128)} %constant.481) | copy-start | bytes 393220
  210.9 53.3 %all-to-all-start.1 = ((f32[3,8,512]{2,0,1:T(4,128)}), f32[3,8,512]{2,0,1:T(4,128)S(1)}, u32[]{:S(2)}, u32[]{:S(2)}) async-start(f32[3,8,512]{2,0,1:T(4,128)} %bitcast.585), calls=%async_computation.1 | async-start | bytes 131072 | tf_op jit(solution)/shard_map/all_to_all | solution.py:171
  217.1 24.3 %copy-start.41 = (f32[512,64,1]{0,1,2:T(8,128)S(1)}, f32[512,64,1]{0,1,2:T(8,128)}, u32[]{:S(2)}) copy-start(f32[512,64,1]{0,1,2:T(8,128)} %constant.483) | copy-start | bytes 393220
  218.0 24.4 %copy-start.39 = (f32[512,64,1]{0,1,2:T(8,128)S(1)}, f32[512,64,1]{0,1,2:T(8,128)}, u32[]{:S(2)}) copy-start(f32[512,64,1]{0,1,2:T(8,128)} %constant.485) | copy-start | bytes 393220
  219.5 18.5 %collective-permute-start.6 = (f32[4,1024]{1,0:T(4,128)}, f32[4,1024]{1,0:T(4,128)}, u32[]{:S(2)}, u32[]{:S(2)}) collective-permute-start(f32[4,1024]{1,0:T(4,128)} %reshape.1114), channel_id=1, source_target_pairs={{0,8},{8,16},{16,24},{1,9},{9,17},{17,25},{2,10},{10,18},{18,26},{... | collective-permute-start | bytes 49160 | tf_op jit(solution)/shard_map/ppermute | solution.py:22
  224.4 16.5 %collective-permute-start.7 = (f32[4,1024]{1,0:T(4,128)S(1)}, f32[4,1024]{1,0:T(4,128)S(1)}, u32[]{:S(2)}, u32[]{:S(2)}) collective-permute-start(f32[4,1024]{1,0:T(4,128)S(1)} %reshape.1116), channel_id=1, source_target_pairs={{8,0},{16,8},{24,16},{9,1},{17,9},{25,17},{10,2},{18,10},{26,18},{... | collective-permute-start | bytes 49160 | tf_op jit(solution)/shard_map/ppermute | solution.py:22
  229.7 11.6 %collective-permute-start.8 = (f32[4,1024]{1,0:T(4,128)S(1)}, f32[4,1024]{1,0:T(4,128)S(1)}, u32[]{:S(2)}, u32[]{:S(2)}) collective-permute-start(f32[4,1024]{1,0:T(4,128)S(1)} %reshape.1118), channel_id=1, source_target_pairs={{0,4},{1,5},{2,6},{3,7},{8,12},{9,13},{10,14},{11,15},{16,20},{17,... | collective-permute-start | bytes 49160 | tf_op jit(solution)/shard_map/ppermute | solution.py:22
  231.5 10.8 %collective-permute-start.9 = (f32[4,1024]{1,0:T(4,128)S(1)}, f32[4,1024]{1,0:T(4,128)S(1)}, u32[]{:S(2)}, u32[]{:S(2)}) collective-permute-start(f32[4,1024]{1,0:T(4,128)S(1)} %reshape.1120), channel_id=1, source_target_pairs={{4,0},{5,1},{6,2},{7,3},{12,8},{13,9},{14,10},{15,11},{20,16},{21,... | collective-permute-start | bytes 49160 | tf_op jit(solution)/shard_map/ppermute | solution.py:22
  235.6 16.3 %collective-permute-start.10 = (f32[4,1024]{1,0:T(4,128)}, f32[4,1024]{1,0:T(4,128)}, u32[]{:S(2)}, u32[]{:S(2)}) collective-permute-start(f32[4,1024]{1,0:T(4,128)} %reshape.1122), channel_id=1, source_target_pairs={{3,0},{0,1},{1,2},{2,3},{7,4},{4,5},{5,6},{6,7},{11,8},{8,9},{9,10... | collective-permute-start | bytes 49160 | tf_op jit(solution)/shard_map/ppermute | solution.py:28
  238.0 25.5 %collective-permute-start.11 = (f32[4,1024]{1,0:T(4,128)}, f32[4,1024]{1,0:T(4,128)}, u32[]{:S(2)}, u32[]{:S(2)}) collective-permute-start(f32[4,1024]{1,0:T(4,128)} %reshape.1124), channel_id=1, source_target_pairs={{1,0},{2,1},{3,2},{0,3},{5,4},{6,5},{7,6},{4,7},{9,8},{10,9},{11,1... | collective-permute-start | bytes 49160 | tf_op jit(solution)/shard_map/ppermute | solution.py:28
  246.3 9.4 %copy-start.2 = (f32[512,512,1]{1,0,2:T(8,128)S(1)}, f32[512,512,1]{1,0,2:T(8,128)}, u32[]{:S(2)}) copy-start(f32[512,512,1]{1,0,2:T(8,128)} %constant.478) | copy-start | bytes 3145732
  246.3 9.5 %copy-start.89 = (pred[64]{0:T(512)(128)(4,1)S(1)}, pred[64]{0:T(512)(128)(4,1)}, u32[]{:S(2)}) copy-start(pred[64]{0:T(512)(128)(4,1)} %get-tuple-element.789) | copy-start | bytes 196
  246.3 9.5 %copy-start.108 = (pred[64]{0:T(512)(128)(4,1)S(1)}, pred[64]{0:T(512)(128)(4,1)}, u32[]{:S(2)}) copy-start(pred[64]{0:T(512)(128)(4,1)} %get-tuple-element.762) | copy-start | bytes 196
  266.2 11.2 %copy-start.62 = (f32[3,2048]{1,0:T(4,128)S(1)}, f32[3,2048]{1,0:T(4,128)}, u32[]{:S(2)}) copy-start(f32[3,2048]{1,0:T(4,128)} %param.50) | copy-start | bytes 73732
  266.2 11.2 %copy-start.63 = (f32[2048]{0:T(1024)S(1)}, f32[2048]{0:T(1024)}, u32[]{:S(2)}) copy-start(f32[2048]{0:T(1024)} %get-tuple-element.744) | copy-start | bytes 24580
  273.7 3.6 collective-permute-start.12
  277.4 17.9 %copy-start.4 = (f32[512,512,1]{1,0,2:T(8,128)S(1)}, f32[512,512,1]{1,0,2:T(8,128)}, u32[]{:S(2)}) copy-start(f32[512,512,1]{1,0,2:T(8,128)} %constant.488) | copy-start | bytes 3145732
  277.5 17.9 %copy-start.19 = (f32[64,4,512]{2,1,0:T(4,128)S(1)}, f32[64,4,512]{2,1,0:T(4,128)}, u32[]{:S(2)}) copy-start(f32[64,4,512]{2,1,0:T(4,128)} %gather_fusion.33) | copy-start | bytes 1572868
  277.5 17.9 %copy-start.91 = (pred[64]{0:T(512)(128)(4,1)S(1)}, pred[64]{0:T(512)(128)(4,1)}, u32[]{:S(2)}) copy-start(pred[64]{0:T(512)(128)(4,1)} %get-tuple-element.754) | copy-start | bytes 196
  277.5 17.9 %copy-start.93 = (pred[64]{0:T(512)(128)(4,1)S(1)}, pred[64]{0:T(512)(128)(4,1)}, u32[]{:S(2)}) copy-start(pred[64]{0:T(512)(128)(4,1)} %get-tuple-element.763) | copy-start | bytes 196
  290.5 11.4 %all-to-all-start.2 = ((f32[8,8,512]{2,0,1:T(8,128)}), f32[8,8,512]{2,0,1:T(8,128)S(1)}, u32[]{:S(2)}, u32[]{:S(2)}) async-start(f32[8,8,512]{2,0,1:T(8,128)} %copy.264), calls=%async_computation.2 | async-start | bytes 262144 | tf_op jit(solution)/shard_map/all_to_all | solution.py:166
  302.6 81.1 %copy-start.109 = (f32[4]{0:T(128)S(1)}, f32[4]{0:T(128)}, u32[]{:S(2)}) copy-start(f32[4]{0:T(128)} %constant.451.clone) | copy-start | bytes 52
  380.0 9.3 %all-to-all-start.3 = ((f32[3,8,512]{2,0,1:T(4,128)}), f32[3,8,512]{2,0,1:T(4,128)S(1)}, u32[]{:S(2)}, u32[]{:S(2)}) async-start(f32[3,8,512]{2,0,1:T(4,128)} %bitcast.109), calls=%async_computation.3 | async-start | bytes 131072 | tf_op jit(solution)/shard_map/all_to_all | solution.py:171
  (63 other events, 137.0 us)
where the time goes:
time: 404 us; the launch traced here: 397 us
  matrix products  169 us (42%)
  local copies, waits for them, and re-layouts  113 us (28%)
  other arithmetic  54.1 us (13%)
  starting transfers between devices  48.7 us (12%)
  waiting for transfers between devices  6.6 us (2%)
    dot_general x64, matrix products, visit(): jnp.einsum('pe,pn->en', pick, sources[component][:, None] * weights, prec...  49.7 us
    dot_general x48, matrix products, basis(): jnp.dot(lagrange(coords[direction]), jnp.asarray(expand_table(direction),...  49.2 us
    dot_general x48, matrix products, visit(): jnp.dot(pick, state[component], precision=highest) * weights  35.2 us
    gather x12, local copies, waits for them, and re-layouts, surface_jump(): own_rows = state[:, local_slot, :].reshape(-1, 512)  22.8 us
    ppermute x8, starting transfers between devices, from_behind(): return lax.ppermute(block, axis, route)  21.2 us
    gather x12, local copies, waits for them, and re-layouts, surface_jump(): far_side = widened[:, far_rank[side], :]  20.2 us
    dot_general x12, matrix products, surface_jump(): jnp.dot(own_rows, transfers[side], precision=highest)  18.3 us
    scatter x2, local copies, waits for them, and re-layouts, coupled_step(): jnp.zeros((8, slots), jnp.float32).at[0].set(-1.0).at[:, slot].set(payload)  15.6 us
  transfers between devices with their start and end apart: 17, of which 2 were waited for; matrix products, arithmetic and copies ran while one was open for 29% of the time, Pallas kernels for 0%

commit v1 on v0

v1 whole, which is shorter than its diff:
```python
import functools
import jax
import jax.numpy as jnp
import numpy as np
from jax import lax
from jax.experimental import pallas as pl
from jax.experimental.pallas import tpu as pltpu
from jax.sharding import PartitionSpec as P

EDGE = 4
node_points = -np.cos(np.pi * np.arange(8) / 7.0)
step_time = 0.1
viscosity = 0.002
penalty = 0.25
couplings = (-0.5, -0.5, -0.5, 0.5)
f32 = jnp.float32
b16 = jnp.bfloat16
MESH = pl.DeviceIdType.MESH


def gap_table():
    differences = node_points[:, None] - node_points[None, :] + np.eye(8)
    inverse = 1.0 / differences
    return inverse * (1.0 - np.eye(8))


def laplace_table():
    differences = node_points[:, None] - node_points[None, :] + np.eye(8)
    weights = 1.0 / np.prod(differences, axis=1)
    derivative = weights[None, :] / weights[:, None] / differences
    derivative = derivative * (1.0 - np.eye(8))
    derivative = derivative - np.eye(8) * derivative.sum(axis=1)[:, None]
    second = derivative @ derivative
    identity = np.eye(8)
    operator = np.kron(np.kron(second, identity), identity)
    operator = operator + np.kron(np.kron(identity, second), identity)
    operator = operator + np.kron(np.kron(identity, identity), second)
    return operator.T


def face_table():
    selection = np.zeros((512, 384))
    for side in range(6):
        edge = 0 if side % 2 == 0 else 7
        for row in range(8):
            for col in range(8):
                if side < 2:
                    node = (edge * 8 + row) * 8 + col
                elif side < 4:
                    node = (row * 8 + edge) * 8 + col
                else:
                    node = (row * 8 + col) * 8 + edge
                selection[node, side * 64 + row * 8 + col] = 1.0
    return selection


def mm(a, b):
    return lax.dot_general(a, b, (((1,), (0,)), ((), ())), preferred_element_type=f32)


def nt(a, b):
    return lax.dot_general(a, b, (((1,), (1,)), ((), ())), preferred_element_type=f32)


def split2(x):
    hi = x.astype(b16)
    return hi, (x - hi.astype(f32)).astype(b16)


def split3(x):
    hi = x.astype(b16)
    rest = x - hi.astype(f32)
    mid = rest.astype(b16)
    return hi, mid, (rest - mid.astype(f32)).astype(b16)


def iota(shape, dim):
    return lax.broadcasted_iota(jnp.int32, shape, dim)


def fiota(shape, dim):
    return iota(shape, dim).astype(f32)


def quotient(x, n):
    return jnp.floor((x + 0.5) * (1.0 / n))


def onehot(mask):
    return jnp.where(mask, 1.0, 0.0).astype(f32)


class Sizes:
    def __init__(self, owners, elements, particles):
        self.owners, self.elements, self.particles = owners, elements, particles
        self.cap = 2 * particles // owners
        self.lw = min(128, self.cap)
        self.bpo = self.cap // self.lw
        self.tiles = owners * self.bpo
        self.rpb = -(-3 * self.bpo // 8) * 8
        self.opc = max(1, 512 // self.cap)
        self.chunk = self.opc * self.cap
        self.tpc = self.opc * self.bpo
        self.chunks = owners // self.opc
        self.edge = EDGE * EDGE


def place(z, cell):
    number = cell.astype(f32)
    device = quotient(number, z.elements)
    element = number - device * z.elements
    owner = device - quotient(device, z.owners) * z.owners
    marks = onehot(fiota((z.owners, z.particles), 0) == owner)
    parts = z.particles // 128
    rows = parts * z.owners
    stacked = jnp.concatenate([marks[:, c * 128 : (c + 1) * 128] for c in range(parts)], axis=0)
    upper = onehot(iota((128, 128), 0) <= iota((128, 128), 1)).astype(b16)
    inside = mm(stacked.astype(b16), upper)
    totals = jnp.broadcast_to(inside[:, 127:128], (rows, 128)).astype(b16)
    row, col = fiota((rows, rows), 0), fiota((rows, rows), 1)
    row_part, col_part = quotient(row, z.owners), quotient(col, z.owners)
    same = (row - row_part * z.owners) == (col - col_part * z.owners)
    earlier = onehot(same & (col_part < row_part)).astype(b16)
    owner_of = fiota((rows, 128), 0)
    owner_of = owner_of - quotient(owner_of, z.owners) * z.owners
    value = stacked * (inside - 1.0 + mm(earlier, totals) + owner_of * z.cap)
    slot = jnp.concatenate(
        [
            jnp.sum(value[c * z.owners : (c + 1) * z.owners], axis=0, keepdims=True)
            for c in range(parts)
        ],
        axis=1,
    )
    return element, slot


def slot_parts(z, slot):
    high = quotient(slot, z.lw)
    low = slot - high * z.lw
    return high, onehot(fiota((z.lw, z.particles), 0) == low).astype(b16)


def pack(z, payload, slot):
    high, low = slot_parts(z, slot)
    three = jnp.concatenate([part.astype(f32) for part in split3(payload)], axis=0)
    spread = jnp.concatenate(
        [jnp.where(high == float(i), three, 0.0).astype(b16) for i in range(z.tiles)], axis=0
    )
    moved = nt(spread, low).reshape(z.tiles, 3, 8, z.lw)
    return moved[:, 0] + moved[:, 1] + moved[:, 2]


def unpack(z, block, slot):
    high, low = slot_parts(z, slot)
    rows = z.owners * z.rpb
    flat = block.reshape(rows, z.lw)
    got = mm(jnp.concatenate(split3(flat), axis=0), low)
    got = got[:rows] + got[rows : 2 * rows] + got[2 * rows :]
    row = fiota((z.rpb, z.particles), 0)
    key = high - (row - quotient(row, z.bpo) * z.bpo)
    total = jnp.zeros((z.rpb, z.particles), f32)
    for o in range(z.owners):
        total = total + jnp.where(
            key == float(o * z.bpo), got[o * z.rpb : (o + 1) * z.rpb], 0.0
        )
    return jnp.concatenate(
        [
            jnp.sum(total[v * z.bpo : (v + 1) * z.bpo], axis=0, keepdims=True)
            for v in range(3)
        ],
        axis=0,
    )


def lagrange(x, table):
    result = None
    for m in range(8):
        factor = (x - float(np.float32(node_points[m]))) * table[:, m : m + 1]
        factor = factor + table[:, 8 + m : 9 + m]
        result = factor if result is None else result * factor
    return result


def basis(coords, table):
    first, second, third = [lagrange(coords[d : d + 1], table) for d in range(3)]
    plane = jnp.concatenate([second[b : b + 1] * third for b in range(8)], axis=0)
    return jnp.concatenate([first[a : a + 1] * plane for a in range(8)], axis=0)


def kernel(
    z, axes, field_ref, nbr_ref, nbr_t_ref, cell_one_ref, ref_one_ref, cell_two_ref, ref_two_ref,
    vel_ref, rate_ref, cut_ref, own_hi_ref, own_lo_ref, sel_ref, sel_t_ref, table_ref,
    field_out_ref, vel_out_ref,
    out_buf, in_buf, ret_out, ret_in, carry_out, carry_in, face_out, face_in,
    w_hi, w_lo, src, force_ref, mid_ref,
    a2a_send, a2a_recv, ret_send, ret_recv, face_send, face_recv, carry_sems,
):
    count_x, count_y, count_z = axes
    ix, iy, iz = lax.axis_index("gx"), lax.axis_index("gy"), lax.axis_index("gz")
    me = iy * count_z + iz
    elements, n_own = z.elements, z.owners
    base = ((ix * n_own + me) * elements).astype(jnp.int32)

    def member(index):
        return (ix, index // count_z, index % count_z)

    def peer(r):
        return lax.rem(me + r, n_own)

    barrier = pltpu.get_barrier_semaphore()

    def greet(r, _):
        pl.semaphore_signal(barrier, inc=1, device_id=member(peer(r)), device_id_type=MESH)
        return 0

    lax.fori_loop(1, n_own, greet, 0)
    up_x = (lax.rem(ix + 1, count_x), iy, iz)
    down_x = (lax.rem(ix + count_x - 1, count_x), iy, iz)
    for device in (up_x, down_x):
        pl.semaphore_signal(barrier, inc=1, device_id=device, device_id_type=MESH)

    def part_copy(stage, r):
        to = peer(r)
        return pltpu.make_async_remote_copy(
            src_ref=out_buf.at[stage, pl.ds(to * z.bpo, z.bpo)],
            dst_ref=in_buf.at[stage, pl.ds(me * z.bpo, z.bpo)],
            send_sem=a2a_send.at[stage, r],
            recv_sem=a2a_recv.at[stage, r],
            device_id=member(to),
            device_id_type=MESH,
        )

    def ret_copy(stage, r):
        to = peer(r)
        return pltpu.make_async_remote_copy(
            src_ref=ret_out.at[stage, to],
            dst_ref=ret_in.at[stage, me],
            send_sem=ret_send.at[stage, r],
            recv_sem=ret_recv.at[stage, r],
            device_id=member(to),
            device_id_type=MESH,
        )

    def start_all(make, stage):
        def body(r, _):
            make(stage, r).start()
            return 0

        lax.fori_loop(1, n_own, body, 0)

    def wait_all(make, stage):
        def body(r, _):
            make(stage, r).wait()
            return 0

        lax.fori_loop(1, n_own, body, 0)

    def send_parts(stage, packed):
        out_buf[stage] = packed
        own = pl.ds(me * z.bpo, z.bpo)
        in_buf[stage, own] = out_buf[stage, own]
        start_all(part_copy, stage)

    def send_back(stage):
        ret_in[stage, me] = ret_out[stage, me]
        start_all(ret_copy, stage)

    face_devices = [
        down_x,
        up_x,
        (ix, lax.rem(iy + count_y - 1, count_y), iz),
        (ix, lax.rem(iy + 1, count_y), iz),
        (ix, iy, lax.rem(iz + count_z - 1, count_z)),
        (ix, iy, lax.rem(iz + 1, count_z)),
    ]

    def face_copy(stage, side):
        return pltpu.make_async_remote_copy(
            src_ref=face_out.at[stage, side],
            dst_ref=face_in.at[stage, side ^ 1],
            send_sem=face_send.at[stage, side],
            recv_sem=face_recv.at[stage, side ^ 1],
            device_id=face_devices[side],
            device_id_type=MESH,
        )

    def face_wait(stage):
        for side in range(6):
            face_copy(stage, side).wait_send()
        for side in range(6):
            pltpu.make_async_remote_copy(
                src_ref=face_out.at[stage, side ^ 1],
                dst_ref=face_in.at[stage, side],
                send_sem=face_send.at[stage, side ^ 1],
                recv_sem=face_recv.at[stage, side],
                device_id=face_devices[side],
                device_id_type=MESH,
            ).wait_recv()

    table = table_ref[...]

    rate = rate_ref[...]
    element, slot_one = place(z, cell_one_ref[...])
    packed = pack(
        z, jnp.concatenate([element + 1.0, ref_one_ref[...], vel_ref[...], rate], axis=0), slot_one
    )
    pl.semaphore_wait(barrier, n_own - 1 + 2)
    send_parts(0, packed)

    square = (elements, elements)
    compacts, partners = [], []
    for side in range(6):
        col = nbr_ref[:, side : side + 1]
        row = nbr_t_ref[side : side + 1, :]
        col_out = (col < base) | (col >= base + elements)
        row_out = (row < base) | (row >= base + elements)
        before = jnp.where(col_out & (iota(square, 0) < iota(square, 1)), 1.0, 0.0)
        before = jnp.sum(before, axis=0, keepdims=True)
        compact = onehot((fiota((z.edge, elements), 0) == before) & row_out).astype(b16)
        compacts.append(jnp.concatenate([compact, compact], axis=1))
        here = onehot(iota(square, 1) == col - base).astype(b16)
        lower = jnp.where(row_out & (row >= 0) & (row < col), 1.0, 0.0)
        rank = jnp.sum(lower, axis=1, keepdims=True)
        far = onehot((fiota((elements, z.edge), 1) == rank) & col_out & (col >= 0)).astype(b16)
        partners.append(jnp.concatenate([here, here, far, far], axis=1))

    def split_state(state):
        return split2(state.reshape(4 * elements, 512))

    def send_faces(stage, hi, lo):
        both = mm(jnp.concatenate([hi, lo], axis=0), sel_ref[...])
        faces = both[: 4 * elements] + both[4 * elements :]
        wide = []
        for side in range(6):
            lanes = jnp.concatenate(
                [
                    faces[k * elements : (k + 1) * elements, side * 64 : (side + 1) * 64]
                    for k in range(4)
                ],
                axis=1,
            )
            pair = jnp.concatenate(split2(lanes), axis=0)
            wide.append(pair)
            face_out[stage, side] = mm(compacts[side], pair)
            face_copy(stage, side).start()
        return wide

    def own_part(state, hi, lo):
        both = mm(jnp.concatenate([hi, lo], axis=0), own_hi_ref[...])
        rows = 4 * elements
        return state + both[:rows] + both[rows:] + mm(hi, own_lo_ref[...])

    def partner_part(stage, wide):
        got = []
        for side in range(6):
            far = jnp.concatenate(split2(face_in[stage, side]), axis=0)
            got.append(mm(partners[side], jnp.concatenate([wide[side ^ 1], far], axis=0)))
        joined = jnp.concatenate(
            [
                jnp.concatenate([got[side][:, k * 64 : (k + 1) * 64] for side in range(6)], axis=1)
                for k in range(4)
            ],
            axis=0,
        )
        hi, lo = split2(joined)
        rows = 4 * elements
        both = mm(jnp.concatenate([hi, lo], axis=0), sel_t_ref[...])
        return penalty * (both[:rows] + both[rows:])

    def chunk_rows(stage, i):
        piece = in_buf[stage, pl.ds(i * z.tpc, z.tpc)]
        return jnp.concatenate([piece[t] for t in range(z.tpc)], axis=1)

    def build(stage, where, i):
        weights = basis(chunk_rows(stage, i)[1:4], table)
        hi, lo = split2(weights)
        w_hi[where, i] = hi
        w_lo[where, i] = lo

    def sample(stage_pos, stage_vel, where, hi, lo, i):
        rows = 3 * elements
        both = mm(jnp.concatenate([hi[:rows], lo[:rows]], axis=0), w_hi[where, i])
        values = both[:rows] + both[rows:] + mm(hi[:rows], w_lo[where, i])
        pos = chunk_rows(stage_pos, i)
        dyn = pos if stage_pos == stage_vel else chunk_rows(stage_vel, i)
        pick = fiota((elements, z.chunk), 0) == pos[0:1] - 1.0
        fluid = jnp.concatenate(
            [
                jnp.sum(
                    jnp.where(pick, values[k * elements : (k + 1) * elements], 0.0),
                    axis=0,
                    keepdims=True,
                )
                for k in range(3)
            ],
            axis=0,
        )
        speeds, rates = dyn[4:7], dyn[7:8]
        offset = fluid - speeds
        accel = rates * offset
        heat = rates * jnp.sum(offset * offset, axis=0, keepdims=True)
        fresh = speeds + step_time * accel
        src[where, i] = jnp.concatenate(
            [couplings[0] * accel, couplings[3] * heat, pos[0:1], fresh], axis=0
        )
        for j in range(z.opc):
            rows = []
            for v in range(3):
                for b in range(z.bpo):
                    at = j * z.cap + b * z.lw
                    rows.append(fresh[v : v + 1, at : at + z.lw])
            if z.rpb > 3 * z.bpo:
                rows.append(jnp.zeros((z.rpb - 3 * z.bpo, z.lw), f32))
            ret_out[where, i * z.opc + j] = jnp.concatenate(rows, axis=0)

    def spread(where, i):
        data = src[where, i]
        pick = fiota((elements, z.chunk), 0) == data[4:5] - 1.0
        loads = jnp.concatenate([jnp.where(pick, data[k : k + 1], 0.0) for k in range(4)], axis=0)
        hi, lo = split2(loads)
        both = nt(w_hi[where, i], jnp.concatenate([hi, lo], axis=0))
        rows = 4 * elements
        force_ref[...] += both[:, :rows] + both[:, rows:] + nt(w_lo[where, i], hi)

    def loop(body):
        def step(i, _):
            body(i)
            return 0

        lax.fori_loop(0, z.chunks, step, 0)

    def forces(where):
        force_ref[...] = jnp.zeros_like(force_ref)
        loop(functools.partial(spread, where))
        return force_ref[...].T

    state = field_ref[...].reshape(4 * elements, 512)
    hi, lo = split2(state)
    wide = send_faces(0, hi, lo)

    element, slot_two = place(z, cell_two_ref[...])
    blank = jnp.zeros((4, z.particles), f32)
    packed = pack(z, jnp.concatenate([element + 1.0, ref_two_ref[...], blank], axis=0), slot_two)
    send_parts(1, packed)

    wait_all(part_copy, 0)

    def first(i):
        build(0, 0, i)
        sample(0, 0, 0, hi, lo, i)

    loop(first)
    send_back(0)
    mid_ref[...] = own_part(state, hi, lo)
    mid_ref[...] += forces(0)
    wait_all(ret_copy, 0)
    carried = jnp.concatenate(
        [unpack(z, ret_in[0], slot_one), rate, jnp.zeros((4, z.particles), f32)], axis=0
    )
    carry_out[...] = carried
    carry = pltpu.make_async_remote_copy(
        src_ref=carry_out,
        dst_ref=carry_in,
        send_sem=carry_sems.at[0],
        recv_sem=carry_sems.at[1],
        device_id=member(lax.rem(me + n_own - 1, n_own)),
        device_id_type=MESH,
    )
    carry.start()
    face_wait(0)
    state = mid_ref[...] + partner_part(0, wide)
    hi, lo = split2(state)
    wide = send_faces(1, hi, lo)
    mid_ref[...] = own_part(state, hi, lo)
    wait_all(part_copy, 1)
    loop(functools.partial(build, 1, 1))
    carry.wait()
    moved = jnp.concatenate([carry_out[...], carry_in[...]], axis=1)
    cut = cut_ref[0]
    bit, width = 1, 2 * z.particles
    while bit < z.particles:
        flag = jnp.full((8, width), (cut // bit) % 2, jnp.int32)
        moved = jnp.where(flag == 1, pltpu.roll(moved, width - bit, 1), moved)
        bit *= 2
    moved = moved[:, : z.particles]
    send_parts(2, pack(z, jnp.concatenate([blank, moved[:4]], axis=0), slot_two))
    wait_all(part_copy, 2)
    loop(functools.partial(sample, 1, 2, 1, hi, lo))
    send_back(1)
    mid_ref[...] += forces(1)
    face_wait(1)
    final = mid_ref[...] + partner_part(1, wide)
    field_out_ref[...] = final.reshape(4, elements, 512)
    wait_all(ret_copy, 1)
    vel_out_ref[...] = unpack(z, ret_in[1], slot_two)


def local(axes, field, neighbours, cell_one, ref_one, cell_two, ref_two, velocity, rate, cut):
    elements, particles = field.shape[1], cell_one.shape[0]
    owners = axes[1] * axes[2]
    z = Sizes(owners, elements, particles)
    selection = face_table()
    own = viscosity * laplace_table() - penalty * np.diag(selection.sum(axis=1))
    own_hi = own.astype(np.float32).astype(b16)
    own_lo = (own - own_hi.astype(np.float64)).astype(np.float32).astype(b16)
    table = np.concatenate([gap_table(), np.eye(8)], axis=1).astype(np.float32)
    vmem = pl.BlockSpec(memory_space=pltpu.VMEM)
    args = [
        field,
        neighbours,
        neighbours.T,
        cell_one[None],
        ref_one,
        cell_two[None],
        ref_two,
        velocity,
        rate[None],
        cut,
        jnp.asarray(own_hi),
        jnp.asarray(own_lo),
        jnp.asarray(selection, b16),
        jnp.asarray(selection.T, b16),
        jnp.asarray(table),
    ]
    specs = [vmem] * len(args)
    specs[9] = pl.BlockSpec(memory_space=pltpu.SMEM)
    dma = pltpu.SemaphoreType.DMA
    return pl.pallas_call(
        functools.partial(kernel, z, axes),
        out_shape=(
            jax.ShapeDtypeStruct(field.shape, f32),
            jax.ShapeDtypeStruct(velocity.shape, f32),
        ),
        in_specs=specs,
        out_specs=(vmem, vmem),
        scratch_shapes=[
            pltpu.VMEM((3, z.tiles, 8, z.lw), f32),
            pltpu.VMEM((3, z.tiles, 8, z.lw), f32),
            pltpu.VMEM((2, owners, z.rpb, z.lw), f32),
            pltpu.VMEM((2, owners, z.rpb, z.lw), f32),
            pltpu.VMEM((8, particles), f32),
            pltpu.VMEM((8, particles), f32),
            pltpu.VMEM((2, 6, z.edge, 256), f32),
            pltpu.VMEM((2, 6, z.edge, 256), f32),
            pltpu.VMEM((2, z.chunks, 512, z.chunk), b16),
            pltpu.VMEM((2, z.chunks, 512, z.chunk), b16),
            pltpu.VMEM((2, z.chunks, 8, z.chunk), f32),
            pltpu.VMEM((512, 4 * elements), f32),
            pltpu.VMEM((4 * elements, 512), f32),
            dma((3, owners)),
            dma((3, owners)),
            dma((2, owners)),
            dma((2, owners)),
            dma((2, 6)),
            dma((2, 6)),
            dma((2,)),
        ],
        compiler_params=pltpu.CompilerParams(
            collective_id=0, has_side_effects=True, vmem_limit_bytes=56 * 1024 * 1024
        ),
    )(*args)


def solution(mesh):
    axes = (mesh.shape["gx"], mesh.shape["gy"], mesh.shape["gz"])
    in_specs = (
        P(None, ("gx", "gy", "gz"), None),
        P(("gx", "gy", "gz"), None),
        P(("gx", "gy", "gz")),
        P(None, ("gx", "gy", "gz")),
        P(("gx", "gy", "gz")),
        P(None, ("gx", "gy", "gz")),
        P(None, ("gx", "gy", "gz")),
        P(("gx", "gy", "gz")),
        P(),
    )
    out_specs = (P(None, ("gx", "gy", "gz"), None), P(None, ("gx", "gy", "gz")))
    return jax.shard_map(
        functools.partial(local, axes), mesh=mesh, in_specs=in_specs, out_specs=out_specs,
        check_vma=False,
    )
```

time: 404 us -> 53.5 us (0.13)
  the two profiles are of different devices: /device:TPU:5 before, /device:TPU:0 now
where the time goes in v1:
time: 53.5 us; the launch traced here: 53.3 us
  Pallas kernels  48.1 us (90%)
  local copies, waits for them, and re-layouts  3.88 us (7%)
  between operations  1.3 us (2%)
    pallas_call x1, Pallas kernels, local(): pl.pallas_call(functools.partial(kernel, z, axes), out_shape=(jax.ShapeDt...  48.1 us
    unnamed x7, local copies, waits for them, and re-layouts  3.88 us

profile of v1, /device:TPU:0, one launch (start us, length us, event | category | flops | bytes accessed | tf_op | source)
XLA Modules:
  0.0 53.3 jit_solution(6242394058832526315)
XLA Ops:
  1.3 0.0 copy-start.1
  1.3 0.7 %copy-done.1 = s32[64,6]{0,1:T(8,128)S(1)} copy-done((s32[64,6]{0,1:T(8,128)S(1)}, s32[64,6]{0,1:T(8,128)}, u32[]{:S(2)}) %copy-start.1) | copy-done | bytes 1560
  2.0 0.7 %copy.16.nbr_ref = s32[64,6]{1,0:T(8,128)} copy(s32[64,6]{0,1:T(8,128)S(1)} %copy-done.1) | data formatting | bytes 3072 | tf_op args[1]
  2.7 48.1 %shard_map.149 = (f32[4,64,512]{2,1,0:T(8,128)}, f32[3,2048]{1,0:T(4,128)}) custom-call(f32[4,64,512]{2,1,0:T(8,128)} %field_ref.1, s32[64,6]{1,0:T(8,128)} %copy.16.nbr_ref, s32[6,64]{1,0:T(8,128)} %bitcast.4, s32[1,2048]{1,0:T(1,128)} %bitcast.5, f32[3,2048]{1,0:T(4,128)} %ref_one_ref.1, s32[1,2048]{1,0:T(1,128)} %bitcast.6, f32[3,2048]{1,0:T(4,128)} %ref_two_ref.1, ...), custom_call_target="tpu_custom_call" | custom-call | tf_op jit(solution)/shard_map/pallas_call | solution.py:528
  50.8 0.0 copy-start
  50.8 1.9 %copy.20 = f32[4,64,512]{2,1,0:T(8,128)} copy(f32[4,64,512]{2,1,0:T(8,128)} %get-tuple-element.4) | data formatting | bytes 1048576
  52.7 0.0 copy-done
  52.7 0.6 %copy.21 = f32[3,2048]{1,0:T(4,128)} copy(f32[3,2048]{1,0:T(4,128)S(1)} %copy-done) | data formatting | bytes 49152
Async XLA Ops:
  1.3 0.7 %copy-start.1 = (s32[64,6]{0,1:T(8,128)S(1)}, s32[64,6]{0,1:T(8,128)}, u32[]{:S(2)}) copy-start(s32[64,6]{0,1:T(8,128)} %param.15) | copy-start | bytes 4612
  50.8 1.9 %copy-start = (f32[3,2048]{1,0:T(4,128)S(1)}, f32[3,2048]{1,0:T(4,128)}, u32[]{:S(2)}) copy-start(f32[3,2048]{1,0:T(4,128)} %get-tuple-element.5) | copy-start | bytes 73732

commit v2 on v1

--- a/solution.py
+++ b/solution.py
@@ -141,21 +141,22 @@
 
 
 def pack(z, payload, slot):
+    fields = payload.shape[0]
     high, low = slot_parts(z, slot)
-    three = jnp.concatenate([part.astype(f32) for part in split3(payload)], axis=0)
+    two = jnp.concatenate([part.astype(f32) for part in split2(payload)], axis=0)
     spread = jnp.concatenate(
-        [jnp.where(high == float(i), three, 0.0).astype(b16) for i in range(z.tiles)], axis=0
-    )
-    moved = nt(spread, low).reshape(z.tiles, 3, 8, z.lw)
-    return moved[:, 0] + moved[:, 1] + moved[:, 2]
+        [jnp.where(high == float(i), two, 0.0) for i in range(z.tiles)], axis=0
+    ).astype(b16)
+    moved = nt(spread, low).reshape(z.tiles, 2 * fields, z.lw)
+    return moved[:, :fields] + moved[:, fields:]
 
 
 def unpack(z, block, slot):
     high, low = slot_parts(z, slot)
     rows = z.owners * z.rpb
     flat = block.reshape(rows, z.lw)
-    got = mm(jnp.concatenate(split3(flat), axis=0), low)
-    got = got[:rows] + got[rows : 2 * rows] + got[2 * rows :]
+    got = mm(jnp.concatenate(split2(flat), axis=0), low)
+    got = got[:rows] + got[rows:]
     row = fiota((z.rpb, z.particles), 0)
     key = high - (row - quotient(row, z.bpo) * z.bpo)
     total = jnp.zeros((z.rpb, z.particles), f32)
@@ -172,6 +173,19 @@
     )
 
 
+def shift(z, pair, cut):
+    bit = 1 << (z.particles - 1).bit_length() - 1
+    while bit >= 1:
+        flag = jnp.full(pair.shape, (cut // bit) % 2, jnp.int32) == 1
+        if bit >= 128:
+            width = z.particles + bit
+            pair = jnp.where(flag[:, :width], pair[:, bit : bit + width], pair[:, :width])
+        else:
+            pair = jnp.where(flag, pltpu.roll(pair, pair.shape[1] - bit, 1), pair)
+        bit //= 2
+    return pair[:, : z.particles]
+
+
 def lagrange(x, table):
     result = None
     for m in range(8):
@@ -188,13 +202,29 @@
 
 
 def kernel(
-    z, axes, field_ref, nbr_ref, nbr_t_ref, cell_one_ref, ref_one_ref, cell_two_ref, ref_two_ref,
-    vel_ref, rate_ref, cut_ref, own_hi_ref, own_lo_ref, sel_ref, sel_t_ref, table_ref,
+    z, axes, field_hbm, nbr_t_ref, cell_one_ref, ref_one_ref, cell_two_ref, ref_two_ref,
+    vel_ref, rate_ref, cut_ref, own_hi_hbm, own_lo_hbm, sel_hbm, sel_t_hbm, table_ref,
     field_out_ref, vel_out_ref,
-    out_buf, in_buf, ret_out, ret_in, carry_out, carry_in, face_out, face_in,
+    field_ref, own_hi_ref, own_lo_ref, sel_ref, sel_t_ref,
+    out_one, in_one, out_two, in_two, ret_out, ret_in, carry_out, carry_in, face_out, face_in,
     w_hi, w_lo, src, force_ref, mid_ref,
-    a2a_send, a2a_recv, ret_send, ret_recv, face_send, face_recv, carry_sems,
+    a2a_send, a2a_recv, ret_send, ret_recv, face_send, face_recv, carry_sems, load_sems,
 ):
+    loads = [
+        pltpu.make_async_copy(here, there, load_sems.at[index])
+        for index, (here, there) in enumerate(
+            [
+                (field_hbm, field_ref),
+                (sel_hbm, sel_ref),
+                (own_hi_hbm, own_hi_ref),
+                (own_lo_hbm, own_lo_ref),
+                (sel_t_hbm, sel_t_ref),
+            ]
+        )
+    ]
+    for load in loads:
+        load.start()
+
     count_x, count_y, count_z = axes
     ix, iy, iz = lax.axis_index("gx"), lax.axis_index("gy"), lax.axis_index("gz")
     me = iy * count_z + iz
@@ -219,11 +249,15 @@
     for device in (up_x, down_x):
         pl.semaphore_signal(barrier, inc=1, device_id=device, device_id_type=MESH)
 
+    def outgoing(stage):
+        return (out_one, in_one) if stage == 0 else (out_two.at[stage - 1], in_two.at[stage - 1])
+
     def part_copy(stage, r):
         to = peer(r)
+        source, target = outgoing(stage)
         return pltpu.make_async_remote_copy(
-            src_ref=out_buf.at[stage, pl.ds(to * z.bpo, z.bpo)],
-            dst_ref=in_buf.at[stage, pl.ds(me * z.bpo, z.bpo)],
+            src_ref=source.at[pl.ds(to * z.bpo, z.bpo)],
+            dst_ref=target.at[pl.ds(me * z.bpo, z.bpo)],
             send_sem=a2a_send.at[stage, r],
             recv_sem=a2a_recv.at[stage, r],
             device_id=member(to),
@@ -256,14 +290,31 @@
         lax.fori_loop(1, n_own, body, 0)
 
     def send_parts(stage, packed):
-        out_buf[stage] = packed
+        source, target = outgoing(stage)
+        source[...] = packed
         own = pl.ds(me * z.bpo, z.bpo)
-        in_buf[stage, own] = out_buf[stage, own]
+        target[own] = source[own]
         start_all(part_copy, stage)
 
-    def send_back(stage):
+    def take(stage, r):
+        if z.opc == 1:
+            part_copy(stage, r).wait()
+
+    def give(stage, r):
+        if z.opc == 1:
+            ret_copy(stage, n_own - r).start()
+
+    def take_all(stage):
+        if z.opc > 1:
+            wait_all(part_copy, stage)
+
+    def give_all(stage):
         ret_in[stage, me] = ret_out[stage, me]
-        start_all(ret_copy, stage)
+        if z.opc > 1:
+            start_all(ret_copy, stage)
+
+    def turn(r):
+        return lax.rem(me + n_own - r, n_own) if z.opc == 1 else r
 
     face_devices = [
         down_x,
@@ -308,17 +359,20 @@
     send_parts(0, packed)
 
     square = (elements, elements)
+    rows = nbr_t_ref[...].astype(f32)
+    columns = jnp.concatenate([rows, rows[:2]], axis=0).T
+    base = base.astype(f32)
     compacts, partners = [], []
     for side in range(6):
-        col = nbr_ref[:, side : side + 1]
-        row = nbr_t_ref[side : side + 1, :]
+        col = columns[:, side : side + 1]
+        row = rows[side : side + 1, :]
         col_out = (col < base) | (col >= base + elements)
         row_out = (row < base) | (row >= base + elements)
         before = jnp.where(col_out & (iota(square, 0) < iota(square, 1)), 1.0, 0.0)
         before = jnp.sum(before, axis=0, keepdims=True)
         compact = onehot((fiota((z.edge, elements), 0) == before) & row_out).astype(b16)
         compacts.append(jnp.concatenate([compact, compact], axis=1))
-        here = onehot(iota(square, 1) == col - base).astype(b16)
+        here = onehot(fiota(square, 1) == col - base).astype(b16)
         lower = jnp.where(row_out & (row >= 0) & (row < col), 1.0, 0.0)
         rank = jnp.sum(lower, axis=1, keepdims=True)
         far = onehot((fiota((elements, z.edge), 1) == rank) & col_out & (col >= 0)).astype(b16)
@@ -367,24 +421,19 @@
         both = mm(jnp.concatenate([hi, lo], axis=0), sel_t_ref[...])
         return penalty * (both[:rows] + both[rows:])
 
-    def chunk_rows(stage, i):
-        piece = in_buf[stage, pl.ds(i * z.tpc, z.tpc)]
+    def chunk_rows(ref, i):
+        piece = ref[pl.ds(i * z.tpc, z.tpc)]
         return jnp.concatenate([piece[t] for t in range(z.tpc)], axis=1)
 
-    def build(stage, where, i):
-        weights = basis(chunk_rows(stage, i)[1:4], table)
-        hi, lo = split2(weights)
-        w_hi[where, i] = hi
-        w_lo[where, i] = lo
-
-    def sample(stage_pos, stage_vel, where, hi, lo, i):
+    def sample(places, hi, lo, i):
+        w_up, w_down = split2(basis(places[1:4], table))
+        w_hi[i] = w_up
+        w_lo[i] = w_down
         rows = 3 * elements
-        both = mm(jnp.concatenate([hi[:rows], lo[:rows]], axis=0), w_hi[where, i])
-        values = both[:rows] + both[rows:] + mm(hi[:rows], w_lo[where, i])
-        pos = chunk_rows(stage_pos, i)
-        dyn = pos if stage_pos == stage_vel else chunk_rows(stage_vel, i)
-        pick = fiota((elements, z.chunk), 0) == pos[0:1] - 1.0
-        fluid = jnp.concatenate(
+        both = mm(jnp.concatenate([hi[:rows], lo[:rows]], axis=0), w_up)
+        values = both[:rows] + both[rows:] + mm(hi[:rows], w_down)
+        pick = fiota((elements, z.chunk), 0) == places[0:1] - 1.0
+        return jnp.concatenate(
             [
                 jnp.sum(
                     jnp.where(pick, values[k * elements : (k + 1) * elements], 0.0),
@@ -395,13 +444,15 @@
             ],
             axis=0,
         )
-        speeds, rates = dyn[4:7], dyn[7:8]
+
+    def drag(stage, fluid, place_row, dynamic, i):
+        speeds, rates = dynamic[:3], dynamic[3:4]
         offset = fluid - speeds
         accel = rates * offset
         heat = rates * jnp.sum(offset * offset, axis=0, keepdims=True)
         fresh = speeds + step_time * accel
-        src[where, i] = jnp.concatenate(
-            [couplings[0] * accel, couplings[3] * heat, pos[0:1], fresh], axis=0
+        src[i] = jnp.concatenate(
+            [couplings[0] * accel, couplings[3] * heat, place_row, fresh], axis=0
         )
         for j in range(z.opc):
             rows = []
@@ -411,53 +462,57 @@
                     rows.append(fresh[v : v + 1, at : at + z.lw])
             if z.rpb > 3 * z.bpo:
                 rows.append(jnp.zeros((z.rpb - 3 * z.bpo, z.lw), f32))
-            ret_out[where, i * z.opc + j] = jnp.concatenate(rows, axis=0)
-
-    def spread(where, i):
-        data = src[where, i]
+            ret_out[stage, i * z.opc + j] = jnp.concatenate(rows, axis=0)
+
+    def spread(i):
+        data = src[i]
         pick = fiota((elements, z.chunk), 0) == data[4:5] - 1.0
         loads = jnp.concatenate([jnp.where(pick, data[k : k + 1], 0.0) for k in range(4)], axis=0)
         hi, lo = split2(loads)
-        both = nt(w_hi[where, i], jnp.concatenate([hi, lo], axis=0))
+        both = nt(w_hi[i], jnp.concatenate([hi, lo], axis=0))
         rows = 4 * elements
-        force_ref[...] += both[:, :rows] + both[:, rows:] + nt(w_lo[where, i], hi)
-
-    def loop(body):
-        def step(i, _):
-            body(i)
-            return 0
-
-        lax.fori_loop(0, z.chunks, step, 0)
-
-    def forces(where):
-        force_ref[...] = jnp.zeros_like(force_ref)
-        loop(functools.partial(spread, where))
-        return force_ref[...].T
-
+        return both[:, :rows] + both[:, rows:] + nt(w_lo[i], hi)
+
+    for load in loads[:2]:
+        load.wait()
     state = field_ref[...].reshape(4 * elements, 512)
     hi, lo = split2(state)
     wide = send_faces(0, hi, lo)
 
     element, slot_two = place(z, cell_two_ref[...])
-    blank = jnp.zeros((4, z.particles), f32)
-    packed = pack(z, jnp.concatenate([element + 1.0, ref_two_ref[...], blank], axis=0), slot_two)
-    send_parts(1, packed)
-
-    wait_all(part_copy, 0)
+    send_parts(
+        1, pack(z, jnp.concatenate([element + 1.0, ref_two_ref[...]], axis=0), slot_two)
+    )
+    for load in loads[2:]:
+        load.wait()
+    mid_ref[...] = own_part(state, hi, lo)
 
     def first(i):
-        build(0, 0, i)
-        sample(0, 0, 0, hi, lo, i)
-
-    loop(first)
-    send_back(0)
+        data = chunk_rows(in_one, i)
+        drag(0, sample(data[:4], hi, lo, i), data[0:1], data[4:], i)
+
+    take_all(0)
+    first(turn(0))
+    force_ref[...] = jnp.zeros_like(force_ref)
+
+    def first_step(r, _):
+        take(0, r)
+        force_ref[...] += spread(turn(r - 1))
+        first(turn(r))
+        give(0, r)
+        return 0
+
+    lax.fori_loop(1, z.chunks, first_step, 0)
+    give_all(0)
+    force = force_ref[...] + spread(turn(z.chunks - 1))
+    mid_ref[...] += force.T
+    face_wait(0)
+    state = mid_ref[...] + partner_part(0, wide)
+    hi, lo = split2(state)
+    wide = send_faces(1, hi, lo)
     mid_ref[...] = own_part(state, hi, lo)
-    mid_ref[...] += forces(0)
     wait_all(ret_copy, 0)
-    carried = jnp.concatenate(
-        [unpack(z, ret_in[0], slot_one), rate, jnp.zeros((4, z.particles), f32)], axis=0
-    )
-    carry_out[...] = carried
+    carry_out[...] = jnp.concatenate([unpack(z, ret_in[0], slot_one), rate], axis=0)
     carry = pltpu.make_async_remote_copy(
         src_ref=carry_out,
         dst_ref=carry_in,
@@ -467,27 +522,40 @@
         device_id_type=MESH,
     )
     carry.start()
-    face_wait(0)
-    state = mid_ref[...] + partner_part(0, wide)
-    hi, lo = split2(state)
-    wide = send_faces(1, hi, lo)
-    mid_ref[...] = own_part(state, hi, lo)
     wait_all(part_copy, 1)
-    loop(functools.partial(build, 1, 1))
+
+    def second(i):
+        places = chunk_rows(in_two.at[0], i)
+        src[i, 0:3] = sample(places, hi, lo, i)
+
+    half = z.chunks // 2
+    for i in range(half):
+        second(i)
     carry.wait()
-    moved = jnp.concatenate([carry_out[...], carry_in[...]], axis=1)
-    cut = cut_ref[0]
-    bit, width = 1, 2 * z.particles
-    while bit < z.particles:
-        flag = jnp.full((8, width), (cut // bit) % 2, jnp.int32)
-        moved = jnp.where(flag == 1, pltpu.roll(moved, width - bit, 1), moved)
-        bit *= 2
-    moved = moved[:, : z.particles]
-    send_parts(2, pack(z, jnp.concatenate([blank, moved[:4]], axis=0), slot_two))
-    wait_all(part_copy, 2)
-    loop(functools.partial(sample, 1, 2, 1, hi, lo))
-    send_back(1)
-    mid_ref[...] += forces(1)
+    moved = shift(z, jnp.concatenate([carry_out[...], carry_in[...]], axis=1), cut_ref[0])
+    send_parts(2, pack(z, moved, slot_two))
+    for i in range(half, z.chunks):
+        second(i)
+    force_ref[...] = jnp.zeros_like(force_ref)
+    take_all(2)
+
+    def finish(i):
+        places = chunk_rows(in_two.at[0], i)
+        drag(1, src[i, 0:3], places[0:1], chunk_rows(in_two.at[1], i), i)
+
+    finish(turn(0))
+
+    def second_step(r, _):
+        take(2, r)
+        finish(turn(r))
+        give(1, r)
+        force_ref[...] += spread(turn(r - 1))
+        return 0
+
+    lax.fori_loop(1, z.chunks, second_step, 0)
+    give_all(1)
+    force = force_ref[...] + spread(turn(z.chunks - 1))
+    mid_ref[...] += force.T
     face_wait(1)
     final = mid_ref[...] + partner_part(1, wide)
     field_out_ref[...] = final.reshape(4, elements, 512)
@@ -507,7 +575,6 @@
     vmem = pl.BlockSpec(memory_space=pltpu.VMEM)
     args = [
         field,
-        neighbours,
         neighbours.T,
         cell_one[None],
         ref_one,
@@ -523,7 +590,9 @@
         jnp.asarray(table),
     ]
     specs = [vmem] * len(args)
-    specs[9] = pl.BlockSpec(memory_space=pltpu.SMEM)
+    specs[8] = pl.BlockSpec(memory_space=pltpu.SMEM)
+    for index in (0, 9, 10, 11, 12):
+        specs[index] = pl.BlockSpec(memory_space=pl.ANY)
     dma = pltpu.SemaphoreType.DMA
     return pl.pallas_call(
         functools.partial(kernel, z, axes),
@@ -534,17 +603,24 @@
         in_specs=specs,
         out_specs=(vmem, vmem),
         scratch_shapes=[
-            pltpu.VMEM((3, z.tiles, 8, z.lw), f32),
-            pltpu.VMEM((3, z.tiles, 8, z.lw), f32),
+            pltpu.VMEM(field.shape, f32),
+            pltpu.VMEM((512, 512), b16),
+            pltpu.VMEM((512, 512), b16),
+            pltpu.VMEM((512, 384), b16),
+            pltpu.VMEM((384, 512), b16),
+            pltpu.VMEM((z.tiles, 8, z.lw), f32),
+            pltpu.VMEM((z.tiles, 8, z.lw), f32),
+            pltpu.VMEM((2, z.tiles, 4, z.lw), f32),
+            pltpu.VMEM((2, z.tiles, 4, z.lw), f32),
             pltpu.VMEM((2, owners, z.rpb, z.lw), f32),
             pltpu.VMEM((2, owners, z.rpb, z.lw), f32),
-            pltpu.VMEM((8, particles), f32),
-            pltpu.VMEM((8, particles), f32),
+            pltpu.VMEM((4, particles), f32),
+            pltpu.VMEM((4, particles), f32),
             pltpu.VMEM((2, 6, z.edge, 256), f32),
             pltpu.VMEM((2, 6, z.edge, 256), f32),
-            pltpu.VMEM((2, z.chunks, 512, z.chunk), b16),
-            pltpu.VMEM((2, z.chunks, 512, z.chunk), b16),
-            pltpu.VMEM((2, z.chunks, 8, z.chunk), f32),
+            pltpu.VMEM((z.chunks, 512, z.chunk), b16),
+            pltpu.VMEM((z.chunks, 512, z.chunk), b16),
+            pltpu.VMEM((z.chunks, 8, z.chunk), f32),
             pltpu.VMEM((512, 4 * elements), f32),
             pltpu.VMEM((4 * elements, 512), f32),
             dma((3, owners)),
@@ -554,6 +630,7 @@
             dma((2, 6)),
             dma((2, 6)),
             dma((2,)),
+            dma((5,)),
         ],
         compiler_params=pltpu.CompilerParams(
             collective_id=0, has_side_effects=True, vmem_limit_bytes=56 * 1024 * 1024

time: 53.5 us -> 42.6 us (0.80)
  Pallas kernels: 48.1 us -> 38.6 us
  local copies, waits for them, and re-layouts: 3.88 us -> 2.49 us
    pallas_call x1, Pallas kernels: 48.1 us -> 38.6 us  [local(): pl.pallas_call(functools.partial(kernel, z, axes), out_shape=(jax.ShapeDt...]
    unnamed x7 -> x4, local copies, waits for them, and re-layouts: 3.88 us -> 2.49 us
where the time goes in v2:
time: 42.6 us; the launch traced here: 42.3 us
  Pallas kernels  38.6 us (91%)
  local copies, waits for them, and re-layouts  2.49 us (6%)
  between operations  1.3 us (3%)
    pallas_call x1, Pallas kernels, local(): pl.pallas_call(functools.partial(kernel, z, axes), out_shape=(jax.ShapeDt...  38.6 us
    unnamed x4, local copies, waits for them, and re-layouts  2.49 us

profile of v2, /device:TPU:0, one launch (start us, length us, event | category | flops | bytes accessed | tf_op | source)
XLA Modules:
  0.0 42.3 jit_solution(17100383528923772700)
XLA Ops:
  1.3 38.6 %shard_map.149 = (f32[4,64,512]{2,1,0:T(8,128)}, f32[3,2048]{1,0:T(4,128)}) custom-call(f32[4,64,512]{2,1,0:T(8,128)} %field_hbm.1, s32[6,64]{1,0:T(8,128)} %bitcast.7, s32[1,2048]{1,0:T(1,128)} %bitcast.4, f32[3,2048]{1,0:T(4,128)} %ref_one_ref.1, s32[1,2048]{1,0:T(1,128)} %bitcast.5, f32[3,2048]{1,0:T(4,128)} %ref_two_ref.1, f32[3,2048]{1,0:T(4,128)} %vel_ref.1, ...), custom_call_target="tpu_custom_call" | custom-call | tf_op jit(solution)/shard_map/pallas_call | solution.py:597
  39.8 0.0 copy-start
  39.8 1.9 %copy.19 = f32[4,64,512]{2,1,0:T(8,128)} copy(f32[4,64,512]{2,1,0:T(8,128)} %get-tuple-element.4) | data formatting | bytes 1048576
  41.7 0.0 copy-done
  41.7 0.6 %copy.20 = f32[3,2048]{1,0:T(4,128)} copy(f32[3,2048]{1,0:T(4,128)S(1)} %copy-done) | data formatting | bytes 49152
Async XLA Ops:
  39.8 1.9 %copy-start = (f32[3,2048]{1,0:T(4,128)S(1)}, f32[3,2048]{1,0:T(4,128)}, u32[]{:S(2)}) copy-start(f32[3,2048]{1,0:T(4,128)} %get-tuple-element.5) | copy-start | bytes 73732

commit v3 on v2

--- a/solution.py
+++ b/solution.py
@@ -88,6 +88,18 @@
 
 def onehot(mask):
     return jnp.where(mask, 1.0, 0.0).astype(f32)
+
+
+def widen(joined, sel_t):
+    rows = joined.shape[0]
+    both = mm(jnp.concatenate(split2(joined), axis=0), sel_t)
+    return penalty * (both[:rows] + both[rows:])
+
+
+def ending(mid_ref, joined_ref, vel_ref, sel_t_ref, field_out_ref, vel_out_ref):
+    final = mid_ref[...] + widen(joined_ref[...], sel_t_ref[...])
+    field_out_ref[...] = final.reshape(field_out_ref.shape)
+    vel_out_ref[...] = vel_ref[...]
 
 
 class Sizes:
@@ -204,10 +216,10 @@
 def kernel(
     z, axes, field_hbm, nbr_t_ref, cell_one_ref, ref_one_ref, cell_two_ref, ref_two_ref,
     vel_ref, rate_ref, cut_ref, own_hi_hbm, own_lo_hbm, sel_hbm, sel_t_hbm, table_ref,
-    field_out_ref, vel_out_ref,
+    mid_ref, joined_ref, vel_out_ref,
     field_ref, own_hi_ref, own_lo_ref, sel_ref, sel_t_ref,
     out_one, in_one, out_two, in_two, ret_out, ret_in, carry_out, carry_in, face_out, face_in,
-    w_hi, w_lo, src, force_ref, mid_ref,
+    w_hi, w_lo, src, flow, force_ref,
     a2a_send, a2a_recv, ret_send, ret_recv, face_send, face_recv, carry_sems, load_sems,
 ):
     loads = [
@@ -404,31 +416,30 @@
         rows = 4 * elements
         return state + both[:rows] + both[rows:] + mm(hi, own_lo_ref[...])
 
-    def partner_part(stage, wide):
+    def partner_faces(stage, wide):
         got = []
         for side in range(6):
             far = jnp.concatenate(split2(face_in[stage, side]), axis=0)
             got.append(mm(partners[side], jnp.concatenate([wide[side ^ 1], far], axis=0)))
-        joined = jnp.concatenate(
+        return jnp.concatenate(
             [
                 jnp.concatenate([got[side][:, k * 64 : (k + 1) * 64] for side in range(6)], axis=1)
                 for k in range(4)
             ],
             axis=0,
         )
-        hi, lo = split2(joined)
-        rows = 4 * elements
-        both = mm(jnp.concatenate([hi, lo], axis=0), sel_t_ref[...])
-        return penalty * (both[:rows] + both[rows:])
 
     def chunk_rows(ref, i):
         piece = ref[pl.ds(i * z.tpc, z.tpc)]
         return jnp.concatenate([piece[t] for t in range(z.tpc)], axis=1)
 
-    def sample(places, hi, lo, i):
+    def build(places, slot):
         w_up, w_down = split2(basis(places[1:4], table))
-        w_hi[i] = w_up
-        w_lo[i] = w_down
+        w_hi[slot] = w_up
+        w_lo[slot] = w_down
+        return w_up, w_down
+
+    def sample(places, hi, lo, w_up, w_down):
         rows = 3 * elements
         both = mm(jnp.concatenate([hi[:rows], lo[:rows]], axis=0), w_up)
         values = both[:rows] + both[rows:] + mm(hi[:rows], w_down)
@@ -445,13 +456,13 @@
             axis=0,
         )
 
-    def drag(stage, fluid, place_row, dynamic, i):
+    def drag(stage, fluid, place_row, dynamic, i, at_src):
         speeds, rates = dynamic[:3], dynamic[3:4]
         offset = fluid - speeds
         accel = rates * offset
         heat = rates * jnp.sum(offset * offset, axis=0, keepdims=True)
         fresh = speeds + step_time * accel
-        src[i] = jnp.concatenate(
+        src[at_src] = jnp.concatenate(
             [couplings[0] * accel, couplings[3] * heat, place_row, fresh], axis=0
         )
         for j in range(z.opc):
@@ -464,14 +475,18 @@
                 rows.append(jnp.zeros((z.rpb - 3 * z.bpo, z.lw), f32))
             ret_out[stage, i * z.opc + j] = jnp.concatenate(rows, axis=0)
 
-    def spread(i):
-        data = src[i]
+    def spread(at_src, at_w):
+        data = src[at_src]
         pick = fiota((elements, z.chunk), 0) == data[4:5] - 1.0
         loads = jnp.concatenate([jnp.where(pick, data[k : k + 1], 0.0) for k in range(4)], axis=0)
         hi, lo = split2(loads)
-        both = nt(w_hi[i], jnp.concatenate([hi, lo], axis=0))
+        both = nt(w_hi[at_w], jnp.concatenate([hi, lo], axis=0))
         rows = 4 * elements
-        return both[:, :rows] + both[:, rows:] + nt(w_lo[i], hi)
+        force = both[:, :rows] + both[:, rows:] + nt(w_lo[at_w], hi)
+        if at_src == 0:
+            force_ref[...] = force
+        else:
+            force_ref[...] += force
 
     for load in loads[:2]:
         load.wait()
@@ -487,27 +502,27 @@
         load.wait()
     mid_ref[...] = own_part(state, hi, lo)
 
-    def first(i):
-        data = chunk_rows(in_one, i)
-        drag(0, sample(data[:4], hi, lo, i), data[0:1], data[4:], i)
+    def first(r):
+        data = chunk_rows(in_one, turn(r))
+        fluid = sample(data[:4], hi, lo, w_hi[r], w_lo[r])
+        drag(0, fluid, data[0:1], data[4:], turn(r), r)
 
     take_all(0)
-    first(turn(0))
-    force_ref[...] = jnp.zeros_like(force_ref)
-
-    def first_step(r, _):
-        take(0, r)
-        force_ref[...] += spread(turn(r - 1))
-        first(turn(r))
-        give(0, r)
-        return 0
-
-    lax.fori_loop(1, z.chunks, first_step, 0)
+    for r in range(z.chunks + 2):
+        if 0 < r < z.chunks:
+            take(0, r)
+        if r >= 2:
+            spread(r - 2, r - 2)
+        if 1 <= r <= z.chunks:
+            first(r - 1)
+        if r < z.chunks:
+            build(chunk_rows(in_one, turn(r))[:4], r)
+        if 1 < r <= z.chunks:
+            give(0, r - 1)
     give_all(0)
-    force = force_ref[...] + spread(turn(z.chunks - 1))
-    mid_ref[...] += force.T
+    mid_ref[...] += force_ref[...].T
     face_wait(0)
-    state = mid_ref[...] + partner_part(0, wide)
+    state = mid_ref[...] + widen(partner_faces(0, wide), sel_t_ref[...])
     hi, lo = split2(state)
     wide = send_faces(1, hi, lo)
     mid_ref[...] = own_part(state, hi, lo)
@@ -526,7 +541,7 @@
 
     def second(i):
         places = chunk_rows(in_two.at[0], i)
-        src[i, 0:3] = sample(places, hi, lo, i)
+        flow[i, 0:3] = sample(places, hi, lo, *build(places, i))
 
     half = z.chunks // 2
     for i in range(half):
@@ -536,29 +551,26 @@
     send_parts(2, pack(z, moved, slot_two))
     for i in range(half, z.chunks):
         second(i)
-    force_ref[...] = jnp.zeros_like(force_ref)
     take_all(2)
 
-    def finish(i):
+    def finish(r):
+        i = turn(r)
         places = chunk_rows(in_two.at[0], i)
-        drag(1, src[i, 0:3], places[0:1], chunk_rows(in_two.at[1], i), i)
-
-    finish(turn(0))
-
-    def second_step(r, _):
-        take(2, r)
-        finish(turn(r))
-        give(1, r)
-        force_ref[...] += spread(turn(r - 1))
-        return 0
-
-    lax.fori_loop(1, z.chunks, second_step, 0)
+        drag(1, flow[i, 0:3], places[0:1], chunk_rows(in_two.at[1], i), i, r)
+
+    for r in range(z.chunks + 1):
+        if 0 < r < z.chunks:
+            take(2, r)
+        if r < z.chunks:
+            finish(r)
+        if r >= 1:
+            spread(r - 1, turn(r - 1))
+        if 0 < r < z.chunks:
+            give(1, r)
     give_all(1)
-    force = force_ref[...] + spread(turn(z.chunks - 1))
-    mid_ref[...] += force.T
+    mid_ref[...] += force_ref[...].T
     face_wait(1)
-    final = mid_ref[...] + partner_part(1, wide)
-    field_out_ref[...] = final.reshape(4, elements, 512)
+    joined_ref[...] = partner_faces(1, wide)
     wait_all(ret_copy, 1)
     vel_out_ref[...] = unpack(z, ret_in[1], slot_two)
 
@@ -594,14 +606,15 @@
     for index in (0, 9, 10, 11, 12):
         specs[index] = pl.BlockSpec(memory_space=pl.ANY)
     dma = pltpu.SemaphoreType.DMA
-    return pl.pallas_call(
+    mid, joined, speeds = pl.pallas_call(
         functools.partial(kernel, z, axes),
         out_shape=(
-            jax.ShapeDtypeStruct(field.shape, f32),
+            jax.ShapeDtypeStruct((4 * elements, 512), f32),
+            jax.ShapeDtypeStruct((4 * elements, 384), f32),
             jax.ShapeDtypeStruct(velocity.shape, f32),
         ),
         in_specs=specs,
-        out_specs=(vmem, vmem),
+        out_specs=(vmem, vmem, vmem),
         scratch_shapes=[
             pltpu.VMEM(field.shape, f32),
             pltpu.VMEM((512, 512), b16),
@@ -621,8 +634,8 @@
             pltpu.VMEM((z.chunks, 512, z.chunk), b16),
             pltpu.VMEM((z.chunks, 512, z.chunk), b16),
             pltpu.VMEM((z.chunks, 8, z.chunk), f32),
+            pltpu.VMEM((z.chunks, 8, z.chunk), f32),
             pltpu.VMEM((512, 4 * elements), f32),
-            pltpu.VMEM((4 * elements, 512), f32),
             dma((3, owners)),
             dma((3, owners)),
             dma((2, owners)),
@@ -636,6 +649,16 @@
             collective_id=0, has_side_effects=True, vmem_limit_bytes=56 * 1024 * 1024
         ),
     )(*args)
+    return pl.pallas_call(
+        ending,
+        out_shape=(
+            jax.ShapeDtypeStruct(field.shape, f32),
+            jax.ShapeDtypeStruct(velocity.shape, f32),
+        ),
+        in_specs=[vmem] * 4,
+        out_specs=(vmem, vmem),
+        compiler_params=pltpu.CompilerParams(vmem_limit_bytes=32 * 1024 * 1024),
+    )(mid, joined, speeds, args[12])
 
 
 def solution(mesh):

time: 42.6 us -> 50 us (1.17); the launches traced: 42.3 us -> 49.2 us
  Pallas kernels: 38.6 us -> 45.1 us
    pallas_call x1, Pallas kernels: 38.6 us -> 43.9 us  [local(): pl.pallas_call(functools.partial(kernel, z, axes), out_shape=(jax.ShapeDt...]
    pallas_call x0 -> x1, Pallas kernels: none -> 1.23 us  [local(): pl.pallas_call(ending, out_shape=(jax.ShapeDtypeStruct(field.shape, f32),...]
    unnamed x4 -> x8, local copies, waits for them, and re-layouts: 2.49 us -> 2.79 us
where the time goes in v3:
time: 50 us; the launch traced here: 49.2 us
  Pallas kernels  45.1 us (90%)
  local copies, waits for them, and re-layouts  2.79 us (6%)
  between operations  1.31 us (3%)
    pallas_call x1, Pallas kernels, local(): pl.pallas_call(functools.partial(kernel, z, axes), out_shape=(jax.ShapeDt...  43.9 us
    unnamed x8, local copies, waits for them, and re-layouts  2.79 us
    pallas_call x1, Pallas kernels, local(): pl.pallas_call(ending, out_shape=(jax.ShapeDtypeStruct(field.shape, f32),...  1.23 us

profile of v3, /device:TPU:0, one launch (start us, length us, event | category | flops | bytes accessed | tf_op | source)
XLA Modules:
  0.0 49.2 jit_solution(18028363819635598748)
XLA Ops:
  1.3 0.0 copy-start
  1.3 43.9 %shard_map.149 = (f32[256,512]{1,0:T(8,128)}, f32[256,384]{1,0:T(8,128)}, f32[3,2048]{1,0:T(4,128)}) custom-call(f32[4,64,512]{2,1,0:T(8,128)} %field_hbm.1, s32[6,64]{1,0:T(8,128)} %bitcast.7, s32[1,2048]{1,0:T(1,128)} %bitcast.4, f32[3,2048]{1,0:T(4,128)} %ref_one_ref.1, s32[1,2048]{1,0:T(1,128)} %bitcast.5, f32[3,2048]{1,0:T(4,128)} %ref_two_ref.1, ...), custom_call_target="tpu_custom_call" | custom-call | tf_op jit(solution)/shard_map/pallas_call | solution.py:609
  45.2 0.0 copy-done
  45.2 0.0 copy-start.1
  45.2 1.0 %copy-done.1 = f32[256,512]{1,0:T(8,128)S(1)} copy-done((f32[256,512]{1,0:T(8,128)S(1)}, f32[256,512]{1,0:T(8,128)}, u32[]{:S(2)}) %copy-start.1) | copy-done | bytes 524312
  46.2 0.0 copy-start.2
  46.2 1.0 %copy-done.2 = f32[256,384]{1,0:T(8,128)S(1)} copy-done((f32[256,384]{1,0:T(8,128)S(1)}, f32[256,384]{1,0:T(8,128)}, u32[]{:S(2)}) %copy-start.2) | copy-done | bytes 393240
  47.2 0.0 copy-start.3
  47.2 0.8 %copy-done.3 = f32[3,2048]{1,0:T(4,128)S(1)} copy-done((f32[3,2048]{1,0:T(4,128)S(1)}, f32[3,2048]{1,0:T(4,128)}, u32[]{:S(2)}) %copy-start.3) | copy-done | bytes 24600
  48.0 1.2 %shard_map.150 = (f32[4,64,512]{2,1,0:T(8,128)}, f32[3,2048]{1,0:T(4,128)}) custom-call(f32[256,512]{1,0:T(8,128)S(1)} %copy-done.1, f32[256,384]{1,0:T(8,128)S(1)} %copy-done.2, f32[3,2048]{1,0:T(4,128)S(1)} %copy-done.3, bf16[384,512]{1,0:T(8,128)(2,1)S(1)} %copy-done), custom_call_target="tpu_custom_call" | custom-call | tf_op jit(solution)/shard_map/pallas_call | solution.py:652
Async XLA Ops:
  1.3 43.9 %copy-start = (bf16[384,512]{1,0:T(8,128)(2,1)S(1)}, bf16[384,512]{1,0:T(8,128)(2,1)}, u32[]{:S(2)}) copy-start(bf16[384,512]{1,0:T(8,128)(2,1)} %constant.13.clone.sel_t_hbm.sel_t_ref) | copy-start | bytes 1179652
  45.2 1.0 %copy-start.1 = (f32[256,512]{1,0:T(8,128)S(1)}, f32[256,512]{1,0:T(8,128)}, u32[]{:S(2)}) copy-start(f32[256,512]{1,0:T(8,128)} %get-tuple-element.5.mid_ref) | copy-start | bytes 1572868
  46.2 1.0 %copy-start.2 = (f32[256,384]{1,0:T(8,128)S(1)}, f32[256,384]{1,0:T(8,128)}, u32[]{:S(2)}) copy-start(f32[256,384]{1,0:T(8,128)} %get-tuple-element.6.joined_ref) | copy-start | bytes 1179652
  47.2 0.8 %copy-start.3 = (f32[3,2048]{1,0:T(4,128)S(1)}, f32[3,2048]{1,0:T(4,128)}, u32[]{:S(2)}) copy-start(f32[3,2048]{1,0:T(4,128)} %get-tuple-element.7.vel_ref) | copy-start | bytes 73732

commit v4 on v3

--- a/solution.py
+++ b/solution.py
@@ -149,40 +149,61 @@
 def slot_parts(z, slot):
     high = quotient(slot, z.lw)
     low = slot - high * z.lw
-    return high, onehot(fiota((z.lw, z.particles), 0) == low).astype(b16)
-
-
-def pack(z, payload, slot):
+    return high, onehot(fiota((z.lw, slot.shape[1]), 0) == low).astype(b16)
+
+
+def over_lanes(z, body, start):
+    step = min(512, z.particles)
+    return lax.fori_loop(
+        0, z.particles // step, lambda c, acc: body(pl.ds(c * step, step), acc), start
+    )
+
+
+def pack(z, payload, rows_ref, slot):
     fields = payload.shape[0]
-    high, low = slot_parts(z, slot)
-    two = jnp.concatenate([part.astype(f32) for part in split2(payload)], axis=0)
-    spread = jnp.concatenate(
-        [jnp.where(high == float(i), two, 0.0) for i in range(z.tiles)], axis=0
-    ).astype(b16)
-    moved = nt(spread, low).reshape(z.tiles, 2 * fields, z.lw)
+    rows_ref[0:fields] = payload
+    rows_ref[8:9] = slot
+
+    def body(lanes, total):
+        high, low = slot_parts(z, rows_ref[8:9, lanes])
+        parts = split2(rows_ref[0:fields, lanes])
+        two = jnp.concatenate([part.astype(f32) for part in parts], axis=0)
+        spread = jnp.concatenate(
+            [jnp.where(high == float(i), two, 0.0) for i in range(z.tiles)], axis=0
+        )
+        return total + nt(spread.astype(b16), low)
+
+    moved = over_lanes(z, body, jnp.zeros((z.tiles * 2 * fields, z.lw), f32))
+    moved = moved.reshape(z.tiles, 2 * fields, z.lw)
     return moved[:, :fields] + moved[:, fields:]
 
 
-def unpack(z, block, slot):
-    high, low = slot_parts(z, slot)
+def unpack(z, block, rows_ref, slot, target_ref):
     rows = z.owners * z.rpb
-    flat = block.reshape(rows, z.lw)
-    got = mm(jnp.concatenate(split2(flat), axis=0), low)
-    got = got[:rows] + got[rows:]
-    row = fiota((z.rpb, z.particles), 0)
-    key = high - (row - quotient(row, z.bpo) * z.bpo)
-    total = jnp.zeros((z.rpb, z.particles), f32)
-    for o in range(z.owners):
-        total = total + jnp.where(
-            key == float(o * z.bpo), got[o * z.rpb : (o + 1) * z.rpb], 0.0
-        )
-    return jnp.concatenate(
-        [
-            jnp.sum(total[v * z.bpo : (v + 1) * z.bpo], axis=0, keepdims=True)
-            for v in range(3)
-        ],
-        axis=0,
-    )
+    flat = jnp.concatenate(split2(block.reshape(rows, z.lw)), axis=0)
+    rows_ref[8:9] = slot
+
+    def body(lanes, _):
+        high, low = slot_parts(z, rows_ref[8:9, lanes])
+        got = mm(flat, low)
+        got = got[:rows] + got[rows:]
+        row = fiota((z.rpb, low.shape[1]), 0)
+        key = high - (row - quotient(row, z.bpo) * z.bpo)
+        total = jnp.zeros(key.shape, f32)
+        for o in range(z.owners):
+            total = total + jnp.where(
+                key == float(o * z.bpo), got[o * z.rpb : (o + 1) * z.rpb], 0.0
+            )
+        target_ref[0:3, lanes] = jnp.concatenate(
+            [
+                jnp.sum(total[v * z.bpo : (v + 1) * z.bpo], axis=0, keepdims=True)
+                for v in range(3)
+            ],
+            axis=0,
+        )
+        return 0
+
+    over_lanes(z, body, 0)
 
 
 def shift(z, pair, cut):
@@ -219,7 +240,7 @@
     mid_ref, joined_ref, vel_out_ref,
     field_ref, own_hi_ref, own_lo_ref, sel_ref, sel_t_ref,
     out_one, in_one, out_two, in_two, ret_out, ret_in, carry_out, carry_in, face_out, face_in,
-    w_hi, w_lo, src, flow, force_ref,
+    w_hi, w_lo, src, flow, force_ref, low_ref,
     a2a_send, a2a_recv, ret_send, ret_recv, face_send, face_recv, carry_sems, load_sems,
 ):
     loads = [
@@ -364,9 +385,8 @@
 
     rate = rate_ref[...]
     element, slot_one = place(z, cell_one_ref[...])
-    packed = pack(
-        z, jnp.concatenate([element + 1.0, ref_one_ref[...], vel_ref[...], rate], axis=0), slot_one
-    )
+    payload = jnp.concatenate([element + 1.0, ref_one_ref[...], vel_ref[...], rate], axis=0)
+    packed = pack(z, payload, low_ref, slot_one)
     pl.semaphore_wait(barrier, n_own - 1 + 2)
     send_parts(0, packed)
 
@@ -456,13 +476,13 @@
             axis=0,
         )
 
-    def drag(stage, fluid, place_row, dynamic, i, at_src):
+    def drag(stage, fluid, place_row, dynamic, i):
         speeds, rates = dynamic[:3], dynamic[3:4]
         offset = fluid - speeds
         accel = rates * offset
         heat = rates * jnp.sum(offset * offset, axis=0, keepdims=True)
         fresh = speeds + step_time * accel
-        src[at_src] = jnp.concatenate(
+        src[i] = jnp.concatenate(
             [couplings[0] * accel, couplings[3] * heat, place_row, fresh], axis=0
         )
         for j in range(z.opc):
@@ -475,18 +495,14 @@
                 rows.append(jnp.zeros((z.rpb - 3 * z.bpo, z.lw), f32))
             ret_out[stage, i * z.opc + j] = jnp.concatenate(rows, axis=0)
 
-    def spread(at_src, at_w):
-        data = src[at_src]
+    def spread(i):
+        data = src[i]
         pick = fiota((elements, z.chunk), 0) == data[4:5] - 1.0
         loads = jnp.concatenate([jnp.where(pick, data[k : k + 1], 0.0) for k in range(4)], axis=0)
         hi, lo = split2(loads)
-        both = nt(w_hi[at_w], jnp.concatenate([hi, lo], axis=0))
+        both = nt(w_hi[i], jnp.concatenate([hi, lo], axis=0))
         rows = 4 * elements
-        force = both[:, :rows] + both[:, rows:] + nt(w_lo[at_w], hi)
-        if at_src == 0:
-            force_ref[...] = force
-        else:
-            force_ref[...] += force
+        force_ref[...] += both[:, :rows] + both[:, rows:] + nt(w_lo[i], hi)
 
     for load in loads[:2]:
         load.wait()
@@ -495,30 +511,30 @@
     wide = send_faces(0, hi, lo)
 
     element, slot_two = place(z, cell_two_ref[...])
-    send_parts(
-        1, pack(z, jnp.concatenate([element + 1.0, ref_two_ref[...]], axis=0), slot_two)
-    )
+    payload = jnp.concatenate([element + 1.0, ref_two_ref[...]], axis=0)
+    send_parts(1, pack(z, payload, low_ref, slot_two))
     for load in loads[2:]:
         load.wait()
     mid_ref[...] = own_part(state, hi, lo)
 
-    def first(r):
-        data = chunk_rows(in_one, turn(r))
-        fluid = sample(data[:4], hi, lo, w_hi[r], w_lo[r])
-        drag(0, fluid, data[0:1], data[4:], turn(r), r)
+    def first(i):
+        data = chunk_rows(in_one, i)
+        fluid = sample(data[:4], hi, lo, *build(data[:4], i))
+        drag(0, fluid, data[0:1], data[4:], i)
 
     take_all(0)
-    for r in range(z.chunks + 2):
-        if 0 < r < z.chunks:
-            take(0, r)
-        if r >= 2:
-            spread(r - 2, r - 2)
-        if 1 <= r <= z.chunks:
-            first(r - 1)
-        if r < z.chunks:
-            build(chunk_rows(in_one, turn(r))[:4], r)
-        if 1 < r <= z.chunks:
-            give(0, r - 1)
+    first(turn(0))
+    force_ref[...] = jnp.zeros_like(force_ref)
+
+    def first_step(r, _):
+        take(0, r)
+        spread(turn(r - 1))
+        first(turn(r))
+        give(0, r)
+        return 0
+
+    lax.fori_loop(1, z.chunks, first_step, 0)
+    spread(turn(z.chunks - 1))
     give_all(0)
     mid_ref[...] += force_ref[...].T
     face_wait(0)
@@ -527,7 +543,8 @@
     wide = send_faces(1, hi, lo)
     mid_ref[...] = own_part(state, hi, lo)
     wait_all(ret_copy, 0)
-    carry_out[...] = jnp.concatenate([unpack(z, ret_in[0], slot_one), rate], axis=0)
+    unpack(z, ret_in[0], low_ref, slot_one, carry_out)
+    carry_out[3:4] = rate
     carry = pltpu.make_async_remote_copy(
         src_ref=carry_out,
         dst_ref=carry_in,
@@ -543,36 +560,43 @@
         places = chunk_rows(in_two.at[0], i)
         flow[i, 0:3] = sample(places, hi, lo, *build(places, i))
 
-    half = z.chunks // 2
-    for i in range(half):
+    def second_places(i, _):
+        @pl.when(i == z.chunks // 2)
+        def _():
+            carry.wait()
+            pair = jnp.concatenate([carry_out[...], carry_in[...]], axis=1)
+            send_parts(2, pack(z, shift(z, pair, cut_ref[0]), low_ref, slot_two))
+
         second(i)
-    carry.wait()
-    moved = shift(z, jnp.concatenate([carry_out[...], carry_in[...]], axis=1), cut_ref[0])
-    send_parts(2, pack(z, moved, slot_two))
-    for i in range(half, z.chunks):
-        second(i)
+        return 0
+
+    lax.fori_loop(0, z.chunks, second_places, 0)
+    force_ref[...] = jnp.zeros_like(force_ref)
     take_all(2)
 
-    def finish(r):
+    def second_step(r, _):
+        @pl.when(r > 0)
+        def _():
+            take(2, r)
+
         i = turn(r)
         places = chunk_rows(in_two.at[0], i)
-        drag(1, flow[i, 0:3], places[0:1], chunk_rows(in_two.at[1], i), i, r)
-
-    for r in range(z.chunks + 1):
-        if 0 < r < z.chunks:
-            take(2, r)
-        if r < z.chunks:
-            finish(r)
-        if r >= 1:
-            spread(r - 1, turn(r - 1))
-        if 0 < r < z.chunks:
+        drag(1, flow[i, 0:3], places[0:1], chunk_rows(in_two.at[1], i), i)
+        spread(i)
+
+        @pl.when(r > 0)
+        def _():
             give(1, r)
+
+        return 0
+
+    lax.fori_loop(0, z.chunks, second_step, 0)
     give_all(1)
     mid_ref[...] += force_ref[...].T
     face_wait(1)
     joined_ref[...] = partner_faces(1, wide)
     wait_all(ret_copy, 1)
-    vel_out_ref[...] = unpack(z, ret_in[1], slot_two)
+    unpack(z, ret_in[1], low_ref, slot_two, vel_out_ref)
 
 
 def local(axes, field, neighbours, cell_one, ref_one, cell_two, ref_two, velocity, rate, cut):
@@ -636,6 +660,7 @@
             pltpu.VMEM((z.chunks, 8, z.chunk), f32),
             pltpu.VMEM((z.chunks, 8, z.chunk), f32),
             pltpu.VMEM((512, 4 * elements), f32),
+            pltpu.VMEM((16, particles), f32),
             dma((3, owners)),
             dma((3, owners)),
             dma((2, owners)),
@@ -657,7 +682,7 @@
         ),
         in_specs=[vmem] * 4,
         out_specs=(vmem, vmem),
-        compiler_params=pltpu.CompilerParams(vmem_limit_bytes=32 * 1024 * 1024),
+        compiler_params=pltpu.CompilerParams(vmem_limit_bytes=56 * 1024 * 1024),
     )(mid, joined, speeds, args[12])
 
 

time: 50 us -> 45 us (0.900); the launches traced: 49.2 us -> 44.8 us
  local copies, waits for them, and re-layouts: 2.79 us -> 0 us
  Pallas kernels: 45.1 us -> 43.5 us
    pallas_call x1, Pallas kernels: 43.9 us -> 41 us  [local(): pl.pallas_call(functools.partial(kernel, z, axes), out_shape=(jax.ShapeDt...]
    unnamed x8 -> x0, local copies, waits for them, and re-layouts: 2.79 us -> none
    pallas_call x1, Pallas kernels: 1.23 us -> 2.52 us  [local(): pl.pallas_call(ending, out_shape=(jax.ShapeDtypeStruct(field.shape, f32),...]
where the time goes in v4:
time: 45 us; the launch traced here: 44.8 us
  Pallas kernels  43.5 us (97%)
  between operations  1.29 us (3%)
    pallas_call x1, Pallas kernels, local(): pl.pallas_call(functools.partial(kernel, z, axes), out_shape=(jax.ShapeDt...  41 us
    pallas_call x1, Pallas kernels, local(): pl.pallas_call(ending, out_shape=(jax.ShapeDtypeStruct(field.shape, f32),...  2.52 us

profile of v4, /device:TPU:0, one launch (start us, length us, event | category | flops | bytes accessed | tf_op | source)
XLA Modules:
  0.0 44.8 jit_solution(14587949694540228776)
XLA Ops:
  1.3 41.0 %shard_map.149 = (f32[256,512]{1,0:T(8,128)}, f32[256,384]{1,0:T(8,128)}, f32[3,2048]{1,0:T(4,128)}) custom-call(f32[4,64,512]{2,1,0:T(8,128)} %field_hbm.1, s32[6,64]{1,0:T(8,128)} %bitcast.7, s32[1,2048]{1,0:T(1,128)} %bitcast.4, f32[3,2048]{1,0:T(4,128)} %ref_one_ref.1, s32[1,2048]{1,0:T(1,128)} %bitcast.5, f32[3,2048]{1,0:T(4,128)} %ref_two_ref.1, ...), custom_call_target="tpu_custom_call" | custom-call | tf_op jit(solution)/shard_map/pallas_call | solution.py:633
  42.3 2.5 %shard_map.150 = (f32[4,64,512]{2,1,0:T(8,128)}, f32[3,2048]{1,0:T(4,128)}) custom-call(f32[256,512]{1,0:T(8,128)} %get-tuple-element.5.mid_ref, f32[256,384]{1,0:T(8,128)} %get-tuple-element.6.joined_ref, f32[3,2048]{1,0:T(4,128)} %get-tuple-element.7.vel_ref, bf16[384,512]{1,0:T(8,128)(2,1)} %constant.13.clone.sel_t_hbm.sel_t_ref), custom_call_target="tpu_custom_call" | custom-call | tf_op jit(solution)/shard_map/pallas_call | solution.py:677

commit v5 on v2

--- a/solution.py
+++ b/solution.py
@@ -88,6 +88,17 @@
 
 def onehot(mask):
     return jnp.where(mask, 1.0, 0.0).astype(f32)
+
+
+def widen(joined, sel_t):
+    rows = joined.shape[0]
+    both = mm(jnp.concatenate(split2(joined), axis=0), sel_t)
+    return penalty * (both[:rows] + both[rows:])
+
+
+def ending(mid_ref, joined_ref, vel_ref, sel_t_ref, field_out_ref, vel_out_ref):
+    field_out_ref[0] = mid_ref[...] + widen(joined_ref[...], sel_t_ref[...])
+    vel_out_ref[...] = vel_ref[...]
 
 
 class Sizes:
@@ -204,10 +215,10 @@
 def kernel(
     z, axes, field_hbm, nbr_t_ref, cell_one_ref, ref_one_ref, cell_two_ref, ref_two_ref,
     vel_ref, rate_ref, cut_ref, own_hi_hbm, own_lo_hbm, sel_hbm, sel_t_hbm, table_ref,
-    field_out_ref, vel_out_ref,
+    mid_ref, joined_ref, vel_out_ref,
     field_ref, own_hi_ref, own_lo_ref, sel_ref, sel_t_ref,
     out_one, in_one, out_two, in_two, ret_out, ret_in, carry_out, carry_in, face_out, face_in,
-    w_hi, w_lo, src, force_ref, mid_ref,
+    w_ref, src, force_ref,
     a2a_send, a2a_recv, ret_send, ret_recv, face_send, face_recv, carry_sems, load_sems,
 ):
     loads = [
@@ -404,22 +415,18 @@
         rows = 4 * elements
         return state + both[:rows] + both[rows:] + mm(hi, own_lo_ref[...])
 
-    def partner_part(stage, wide):
+    def partner_faces(stage, wide):
         got = []
         for side in range(6):
             far = jnp.concatenate(split2(face_in[stage, side]), axis=0)
             got.append(mm(partners[side], jnp.concatenate([wide[side ^ 1], far], axis=0)))
-        joined = jnp.concatenate(
+        return jnp.concatenate(
             [
                 jnp.concatenate([got[side][:, k * 64 : (k + 1) * 64] for side in range(6)], axis=1)
                 for k in range(4)
             ],
             axis=0,
         )
-        hi, lo = split2(joined)
-        rows = 4 * elements
-        both = mm(jnp.concatenate([hi, lo], axis=0), sel_t_ref[...])
-        return penalty * (both[:rows] + both[rows:])
 
     def chunk_rows(ref, i):
         piece = ref[pl.ds(i * z.tpc, z.tpc)]
@@ -427,8 +434,8 @@
 
     def sample(places, hi, lo, i):
         w_up, w_down = split2(basis(places[1:4], table))
-        w_hi[i] = w_up
-        w_lo[i] = w_down
+        w_ref[i, 0:512] = w_up
+        w_ref[i, 512:1024] = w_down
         rows = 3 * elements
         both = mm(jnp.concatenate([hi[:rows], lo[:rows]], axis=0), w_up)
         values = both[:rows] + both[rows:] + mm(hi[:rows], w_down)
@@ -469,9 +476,8 @@
         pick = fiota((elements, z.chunk), 0) == data[4:5] - 1.0
         loads = jnp.concatenate([jnp.where(pick, data[k : k + 1], 0.0) for k in range(4)], axis=0)
         hi, lo = split2(loads)
-        both = nt(w_hi[i], jnp.concatenate([hi, lo], axis=0))
-        rows = 4 * elements
-        return both[:, :rows] + both[:, rows:] + nt(w_lo[i], hi)
+        both = nt(w_ref[i], hi)
+        return both[:512] + both[512:] + nt(w_ref[i, 0:512], lo)
 
     for load in loads[:2]:
         load.wait()
@@ -507,7 +513,7 @@
     force = force_ref[...] + spread(turn(z.chunks - 1))
     mid_ref[...] += force.T
     face_wait(0)
-    state = mid_ref[...] + partner_part(0, wide)
+    state = mid_ref[...] + widen(partner_faces(0, wide), sel_t_ref[...])
     hi, lo = split2(state)
     wide = send_faces(1, hi, lo)
     mid_ref[...] = own_part(state, hi, lo)
@@ -548,8 +554,8 @@
     def second_step(r, _):
         take(2, r)
         finish(turn(r))
+        force_ref[...] += spread(turn(r - 1))
         give(1, r)
-        force_ref[...] += spread(turn(r - 1))
         return 0
 
     lax.fori_loop(1, z.chunks, second_step, 0)
@@ -557,8 +563,7 @@
     force = force_ref[...] + spread(turn(z.chunks - 1))
     mid_ref[...] += force.T
     face_wait(1)
-    final = mid_ref[...] + partner_part(1, wide)
-    field_out_ref[...] = final.reshape(4, elements, 512)
+    joined_ref[...] = partner_faces(1, wide)
     wait_all(ret_copy, 1)
     vel_out_ref[...] = unpack(z, ret_in[1], slot_two)
 
@@ -594,14 +599,15 @@
     for index in (0, 9, 10, 11, 12):
         specs[index] = pl.BlockSpec(memory_space=pl.ANY)
     dma = pltpu.SemaphoreType.DMA
-    return pl.pallas_call(
+    mid, joined, speeds = pl.pallas_call(
         functools.partial(kernel, z, axes),
         out_shape=(
-            jax.ShapeDtypeStruct(field.shape, f32),
+            jax.ShapeDtypeStruct((4 * elements, 512), f32),
+            jax.ShapeDtypeStruct((4 * elements, 384), f32),
             jax.ShapeDtypeStruct(velocity.shape, f32),
         ),
         in_specs=specs,
-        out_specs=(vmem, vmem),
+        out_specs=(vmem, vmem, vmem),
         scratch_shapes=[
             pltpu.VMEM(field.shape, f32),
             pltpu.VMEM((512, 512), b16),
@@ -618,11 +624,9 @@
             pltpu.VMEM((4, particles), f32),
             pltpu.VMEM((2, 6, z.edge, 256), f32),
             pltpu.VMEM((2, 6, z.edge, 256), f32),
-            pltpu.VMEM((z.chunks, 512, z.chunk), b16),
-            pltpu.VMEM((z.chunks, 512, z.chunk), b16),
+            pltpu.VMEM((z.chunks, 1024, z.chunk), b16),
             pltpu.VMEM((z.chunks, 8, z.chunk), f32),
             pltpu.VMEM((512, 4 * elements), f32),
-            pltpu.VMEM((4 * elements, 512), f32),
             dma((3, owners)),
             dma((3, owners)),
             dma((2, owners)),
@@ -636,6 +640,23 @@
             collective_id=0, has_side_effects=True, vmem_limit_bytes=56 * 1024 * 1024
         ),
     )(*args)
+    whole = pl.BlockSpec(velocity.shape, lambda k: (0, 0))
+    return pl.pallas_call(
+        ending,
+        grid=(4,),
+        out_shape=(
+            jax.ShapeDtypeStruct(field.shape, f32),
+            jax.ShapeDtypeStruct(velocity.shape, f32),
+        ),
+        in_specs=[
+            pl.BlockSpec((elements, 512), lambda k: (k, 0)),
+            pl.BlockSpec((elements, 384), lambda k: (k, 0)),
+            whole,
+            pl.BlockSpec((384, 512), lambda k: (0, 0)),
+        ],
+        out_specs=(pl.BlockSpec((1, elements, 512), lambda k: (k, 0, 0)), whole),
+        compiler_params=pltpu.CompilerParams(vmem_limit_bytes=56 * 1024 * 1024),
+    )(mid, joined, speeds, args[12])
 
 
 def solution(mesh):

time: 42.6 us -> 44.1 us (1.035)
  Pallas kernels: 38.6 us -> 42.6 us
  local copies, waits for them, and re-layouts: 2.49 us -> 0 us
    pallas_call x0 -> x1, Pallas kernels: none -> 3.89 us  [local(): pl.pallas_call(ending, grid=(4,), out_shape=(jax.ShapeDtypeStruct(field.s...]
    unnamed x4 -> x0, local copies, waits for them, and re-layouts: 2.49 us -> none
where the time goes in v5:
time: 44.1 us; the launch traced here: 43.9 us
  Pallas kernels  42.6 us (97%)
  between operations  1.29 us (3%)
    pallas_call x1, Pallas kernels, local(): pl.pallas_call(functools.partial(kernel, z, axes), out_shape=(jax.ShapeDt...  38.7 us
    pallas_call x1, Pallas kernels, local(): pl.pallas_call(ending, grid=(4,), out_shape=(jax.ShapeDtypeStruct(field.s...  3.89 us

profile of v5, /device:TPU:0, one launch (start us, length us, event | category | flops | bytes accessed | tf_op | source)
XLA Modules:
  0.0 43.9 jit_solution(11108969178182097578)
XLA Ops:
  1.3 38.7 %shard_map.149 = (f32[256,512]{1,0:T(8,128)}, f32[256,384]{1,0:T(8,128)}, f32[3,2048]{1,0:T(4,128)}) custom-call(f32[4,64,512]{2,1,0:T(8,128)} %field_hbm.1, s32[6,64]{1,0:T(8,128)} %bitcast.7, s32[1,2048]{1,0:T(1,128)} %bitcast.4, f32[3,2048]{1,0:T(4,128)} %ref_one_ref.1, s32[1,2048]{1,0:T(1,128)} %bitcast.5, f32[3,2048]{1,0:T(4,128)} %ref_two_ref.1, ...), custom_call_target="tpu_custom_call" | custom-call | tf_op jit(solution)/shard_map/pallas_call | solution.py:602
  40.0 3.9 %shard_map.150 = (f32[4,64,512]{2,1,0:T(8,128)}, f32[3,2048]{1,0:T(4,128)}) custom-call(f32[256,512]{1,0:T(8,128)} %get-tuple-element.5.mid_ref, f32[256,384]{1,0:T(8,128)} %get-tuple-element.6.joined_ref, f32[3,2048]{1,0:T(4,128)} %get-tuple-element.7.vel_ref, bf16[384,512]{1,0:T(8,128)(2,1)} %constant.13.clone.sel_t_hbm.sel_t_ref), custom_call_target="tpu_custom_call" | custom-call | tf_op jit(solution)/shard_map/pallas_call | solution.py:644
